TPU v7x, 256 devices: a whole 4x4x8 slice. The times are simulated.
256 devices in a mesh: section: 8 (over z_hi, y), seq: 32 (over z_lo, x, core).
Axes of the slice: x: 4, y: 4, z: 8 (z_hi: 2, z_lo: 4; z = z_hi * 4 + z_lo), core: 2. Of those that a mesh axis runs over, the one named last changes fastest.
Arguments:
- latents: bfloat16 [8, 4096, 1408], P('section', 'seq'), may hold values from -6 to 6
- skip_weight: bfloat16 [8, 1408, 1408], P('section'), may hold values from -0.109375 to 0.109375
- project_in: bfloat16 [8, 1408, 2112], P('section'), as said below
- project_out: bfloat16 [8, 704, 1408], P('section'), may hold values from -0.21875 to 0.21875
- upstream: bfloat16 [8, 4096, 1408], P('section', 'seq'), may hold values from -6 to 6
Outputs:
- block_out: bfloat16 [8, 4096, 1408], P('section', 'seq')
- grad_latents: bfloat16 [8, 4096, 1408], P('section', 'seq')
Inputs may be any that keep to these rules, and one draw needn't show every extreme that they name: project_in is a dense projection matrix.
All inputs are finite; a program needn't handle non-finite values.
Results may differ from a plain program's by a relative error of at most 0.028.
Values may be sent and summed in bfloat16 or wider, within the bound.
A program may use at most 192 MiB of HBM per device.

v0:
```python
import math

import jax
import jax.numpy as jnp
from jax import lax
from jax.sharding import PartitionSpec as P

HEADS = 8


EPSILON = 1e-06


def layer_norm(vector):
    center = vector - jnp.mean(vector, -1, keepdims=True)
    spread = jnp.mean(center * center, -1, keepdims=True)
    return center * lax.rsqrt(spread + EPSILON)


def mirror_skip(payload):
    section_count = lax.axis_size("section")
    pieces = payload.reshape((section_count, payload.shape[0] // section_count, payload.shape[1]))
    spread = lax.all_to_all(pieces, "section", split_axis=0, concat_axis=0, tiled=True)
    settled = lax.all_to_all(
        jnp.flip(spread, 0), "section", split_axis=0, concat_axis=0, tiled=True
    )
    return settled.reshape(payload.shape)


def mirror_grad(payload):
    section_count = lax.axis_size("section")
    pieces = payload.reshape((section_count, payload.shape[0] // section_count, payload.shape[1]))
    spread = lax.all_to_all(pieces, "section", split_axis=0, concat_axis=0, tiled=True)
    settled = lax.all_to_all(
        jnp.flip(spread, 0), "section", split_axis=0, concat_axis=0, tiled=True
    )
    return settled.reshape(payload.shape)


def body(latents, skip_weight, project_in, project_out, upstream):
    section_count = lax.axis_size("section")
    is_upper = lax.axis_index("section") >= section_count // 2
    inputs = latents[0]
    weight = skip_weight[0]
    weight_in = project_in[0]
    weight_out = project_out[0]
    gradient = upstream[0]
    tok_rows = inputs.shape[0]
    head_width = weight_out.shape[0]
    head_count = HEADS
    head_depth = head_width // head_count
    score_scale = 1.0 / math.sqrt(head_depth)
    projected = jnp.dot(inputs, weight, preferred_element_type=jnp.float32)
    payload = jnp.where(is_upper, jnp.zeros_like(projected), projected).astype(jnp.bfloat16)
    arrived = mirror_skip(payload)
    mixed_sum = projected + arrived.astype(jnp.float32)
    joined_value, mix_back = jax.vjp(layer_norm, mixed_sum)
    block_input = jnp.where(is_upper, joined_value.astype(jnp.bfloat16), inputs)
    normed, norm_back = jax.vjp(layer_norm, block_input.astype(jnp.float32))
    projections = jnp.dot(
        normed.astype(jnp.bfloat16), weight_in, preferred_element_type=jnp.float32
    ).astype(jnp.bfloat16)
    queries = projections[:, :head_width].reshape(tok_rows, head_count, head_depth)
    key_local = projections[:, head_width : 2 * head_width].reshape(
        tok_rows, head_count, head_depth
    )
    value_local = projections[:, 2 * head_width :].reshape(tok_rows, head_count, head_depth)
    gathered_keys, gathered_values = (
        lax.all_gather(key_local, "seq", axis=0, tiled=True),
        lax.all_gather(value_local, "seq", axis=0, tiled=True),
    )
    scores = (
        jnp.einsum("rhd,lhd->hrl", queries, gathered_keys, preferred_element_type=jnp.float32)
        * score_scale
    )
    row_top = jnp.max(scores, -1)
    lifted_rows = jnp.exp(scores - row_top[:, :, None])
    row_total = jnp.sum(lifted_rows, -1)
    attention = lifted_rows / row_total[:, :, None]
    rounded = attention.astype(jnp.bfloat16)
    attended = jnp.einsum(
        "hrl,lhd->rhd", rounded, gathered_values, preferred_element_type=jnp.float32
    ).astype(jnp.bfloat16)
    block_out = (
        block_input.astype(jnp.float32)
        + jnp.dot(
            attended.reshape(tok_rows, head_width), weight_out, preferred_element_type=jnp.float32
        )
    ).astype(jnp.bfloat16)
    grad_att = jnp.dot(gradient, weight_out.T, preferred_element_type=jnp.float32).astype(
        jnp.bfloat16
    )
    grad_heads = grad_att.reshape(tok_rows, head_count, head_depth)
    row_delta = jnp.sum(grad_heads.astype(jnp.float32) * attended.astype(jnp.float32), -1)
    grad_prob = jnp.einsum(
        "rhd,lhd->hrl", grad_heads, gathered_values, preferred_element_type=jnp.float32
    )
    grad_score = (attention * (grad_prob - row_delta.T[:, :, None]) * score_scale).astype(
        jnp.bfloat16
    )
    grad_q = jnp.einsum(
        "hrl,lhd->rhd", grad_score, gathered_keys, preferred_element_type=jnp.float32
    ).astype(jnp.bfloat16)
    weight_stack = jnp.stack([grad_score, rounded])
    row_stack = jnp.stack([queries, grad_heads])
    partials = jnp.einsum(
        "giyx,gyio->xgio", weight_stack, row_stack, preferred_element_type=jnp.float32
    )
    partials = partials.reshape(gathered_keys.shape[0], 2 * head_width)
    owned_rows = lax.psum_scatter(
        partials.astype(jnp.bfloat16), "seq", scatter_dimension=0, tiled=True
    ).astype(jnp.float32)
    grad_proj = jnp.concatenate(
        [
            grad_q.reshape(tok_rows, head_width),
            owned_rows[:, :head_width].astype(jnp.bfloat16),
            owned_rows[:, head_width:].astype(jnp.bfloat16),
        ],
        axis=1,
    )
    grad_normed = jnp.dot(grad_proj, weight_in.T, preferred_element_type=jnp.float32)
    grad_input = gradient.astype(jnp.float32) + norm_back(grad_normed)[0]
    grad_mixed = mix_back(grad_input)[0]
    sent_back = jnp.where(is_upper, grad_mixed, jnp.zeros_like(grad_mixed)).astype(jnp.bfloat16)
    returned = mirror_grad(sent_back)
    back_term = jnp.where(is_upper, sent_back, returned)
    through = jnp.dot(back_term, weight.T, preferred_element_type=jnp.float32)
    grad_latents = jnp.where(is_upper, through, grad_input + through).astype(jnp.bfloat16)
    return (block_out[None], grad_latents[None])


def solution(mesh):
    return jax.shard_map(
        body,
        mesh=mesh,
        in_specs=(
            P("section", "seq", None),
            P("section", None, None),
            P("section", None, None),
            P("section", None, None),
            P("section", "seq", None),
        ),
        out_specs=(P("section", "seq", None), P("section", "seq", None)),
        check_vma=False,
    )
```

profile of v0, /device:TPU:8, one launch (start us, length us, event | category | flops | bytes accessed | tf_op | source)
XLA Modules:
  0.0 476.8 jit_solution(13128498068280594584)
XLA Ops:
  7.2 3.2 select_convert_fusion.1
  10.4 22.2 %all_to_all.20 = bf16[8,16,1408]{2,1,0:T(8,128)(2,1)S(1)} all-to-all(bf16[8,16,1408]{2,1,0:T(8,128)(2,1)S(1)} %bitcast.106), channel_id=1, replica_groups=mesh['section'=8,'seq'=32] {'section'}, dimensions={0} | all-to-all | bytes 720896 | tf_op jit(solution)/shard_map/all_to_all | solution.py:23
  33.4 18.3 %all_to_all.21 = bf16[8,16,1408]{2,1,0:T(8,128)(2,1)S(1)} all-to-all(bf16[8,16,1408]{2,1,0:T(8,128)(2,1)} %rev.7), channel_id=1, replica_groups=mesh['section'=8,'seq'=32] {'section'}, dimensions={0} | all-to-all | bytes 720896 | tf_op jit(solution)/shard_map/all_to_all | solution.py:24
  52.2 1.3 convert_reduce_fusion
  53.7 4.5 fusion.21
  60.0 2.3 fusion.31
  62.3 71.4 %all-gather.5.cloned.1.call-done = bf16[4096,8,88]{0,2,1:T(8,128)(2,1)} async-done(((bf16[128,8,88]{0,2,1:T(8,128)(2,1)}), bf16[4096,8,88]{0,2,1:T(8,128)(2,1)}) %all-gather.5.cloned.1.call-update) | async-done | bytes 5767184 | tf_op jit(solution)/shard_map/all_gather | solution.py:69
  133.8 10.7 %fusion.71 = (f32[8,128]{1,0:T(8,128)S(1)}, f32[8,128,4096]{2,1,0:T(8,128)}) fusion(bf16[128,8,88]{0,2,1:T(8,128)(2,1)} %bitcast.109, bf16[4096,8,88]{0,2,1:T(8,128)(2,1)} %all-gather.5.cloned.1.call-done), kind=kOutput, calls=%fused_computation.83 | convolution fusion | flops 750784512 | bytes 22728704 | tf_op jit(solution)/shard_map/sub | solution.py:77
  144.5 9.6 %fusion.84 = bf16[1,8,128,4096]{3,2,1,0:T(8,128)(2,1)} fusion(f32[8,128,4096]{2,1,0:T(8,128)} %get-tuple-element.14, f32[8,128]{1,0:T(8,128)S(1)} %get-tuple-element.13), kind=kLoop, calls=%fused_computation.84 | loop fusion | flops 8388608 | bytes 25169920 | tf_op jit(solution)/shard_map/stack | solution.py:104
  154.1 56.8 %all-gather.3.cloned.1.call-done = bf16[4096,8,88]{0,2,1:T(8,128)(2,1)} async-done(((bf16[128,8,88]{0,2,1:T(8,128)(2,1)}), bf16[4096,8,88]{0,2,1:T(8,128)(2,1)}) %all-gather.3.cloned.1.call-update) | async-done | bytes 5767184 | tf_op jit(solution)/shard_map/all_gather | solution.py:70
  210.9 11.0 %multiply_reduce_fusion.3 = (f32[128,8]{0,1:T(8,128)S(1)}, bf16[8,88,128]{2,1,0:T(8,128)(2,1)}) fusion(bf16[128,8,88]{0,2,1:T(8,128)(2,1)} %bitcast.113, bf16[4096,8,88]{0,2,1:T(8,128)(2,1)} %all-gather.3.cloned.1.call-done, f32[8,128,4096]{2,1,0:T(8,128)} %get-tuple-element.14, f32[8,128]{1,0:T(8,128)S(1)} %get-tuple-element.13), kind=kOutput, calls=%fused_computation.63 | convolution fusion | flops 747035648 | bytes 22913024 | tf_op jit(solution)/shard_map/hrl,lhd->rhd/dot_general | solution.py:81
  221.9 12.5 %multiply_convert_fusion = bf16[8,128,4096]{2,1,0:T(8,128)(2,1)} fusion(bf16[128,8,88]{0,2,1:T(8,128)(2,1)S(1)} %bitcast.114, bf16[4096,8,88]{0,2,1:T(8,128)(2,1)} %all-gather.3.cloned.1.call-done, f32[8,128]{1,0:T(8,128)S(1)} %bitcast.116, f32[8,128,4096]{2,1,0:T(8,128)} %get-tuple-element.14, f32[8,128]{1,0:T(8,128)S(1)} %get-tuple-element.13), kind=kOutput, calls=%fused_computation.5 | convolution fusion | flops 759169024 | bytes 31121408 | tf_op jit(solution)/shard_map/rhd,lhd->hrl/dot_general | solution.py:95
  234.4 10.0 %fusion.8 = bf16[2,8,88,4096]{3,2,1,0:T(8,128)(2,1)} fusion(bf16[1,8,128,4096]{3,2,1,0:T(8,128)(2,1)} %fusion.84, bf16[1,8,128,4096]{3,2,1,0:T(8,128)(2,1)} %bitcast.104, bf16[1,128,8,88]{1,3,2,0:T(8,128)(2,1)S(1)} %bitcast.115, bf16[1,128,8,88]{1,3,2,0:T(8,128)(2,1)S(1)} %bitcast.110), kind=kOutput, calls=%fused_computation.9 | convolution fusion | flops 1490731008 | bytes 28672000 | tf_op jit(solution)/shard_map/giyx,gyio->xgio/dot_general | solution.py:106
  244.4 15.2 %copy.7 = bf16[4096,1408]{1,0:T(8,128)(2,1)} copy(bf16[4096,1408]{0,1:T(8,128)(2,1)} %bitcast.103) | data formatting | bytes 23068672
  259.6 8.6 %convolution_convert_fusion = bf16[8,88,128]{2,1,0:T(8,128)(2,1)} fusion(bf16[4096,8,88]{0,2,1:T(8,128)(2,1)} %all-gather.5.cloned.1.call-done, bf16[8,128,4096]{2,1,0:T(8,128)(2,1)} %multiply_convert_fusion), kind=kOutput, calls=%fused_computation.30 | convolution fusion | flops 738287616 | bytes 14336000 | tf_op jit(solution)/shard_map/hrl,lhd->rhd/dot_general | solution.py:101
  268.2 155.8 %reduce-scatter.4.cloned.1.call-done = bf16[128,1408]{1,0:T(8,128)(2,1)} async-done(((bf16[4096,1408]{1,0:T(8,128)(2,1)}), bf16[128,1408]{1,0:T(8,128)(2,1)}) %reduce-scatter.4.cloned.1.call-update) | async-done | bytes 360464
  423.9 1.9 copy.8
  425.8 4.2 fusion.48
  432.2 17.2 %all_to_all.22 = bf16[8,16,1408]{2,1,0:T(8,128)(2,1)S(1)} all-to-all(bf16[8,16,1408]{2,1,0:T(8,128)(2,1)S(1)} %bitcast.105), channel_id=1, replica_groups=mesh['section'=8,'seq'=32] {'section'}, dimensions={0} | all-to-all | bytes 720896 | tf_op jit(solution)/shard_map/all_to_all | solution.py:33
  450.2 4.8 %all-to-all-start.3 = ((bf16[8,16,1408]{2,1,0:T(8,128)(2,1)}), bf16[8,16,1408]{2,1,0:T(8,128)(2,1)S(1)}, u32[]{:S(2)}, u32[]{:S(2)}) async-start(bf16[8,16,1408]{2,1,0:T(8,128)(2,1)} %rev.8), calls=%async_computation.3 | async-start | bytes 720896 | tf_op jit(solution)/shard_map/all_to_all | solution.py:34
  455.0 2.2 fusion.25
  457.1 7.5 %all-to-all-done.3 = bf16[8,16,1408]{2,1,0:T(8,128)(2,1)S(1)} async-done(((bf16[8,16,1408]{2,1,0:T(8,128)(2,1)}), bf16[8,16,1408]{2,1,0:T(8,128)(2,1)S(1)}, u32[]{:S(2)}, u32[]{:S(2)}) %all-to-all-start.3) | async-done | bytes 360480 | tf_op jit(solution)/shard_map/all_to_all | solution.py:34
  464.6 1.3 bitcast_select_fusion
  465.9 4.4 fusion.39
  (36 shorter events, 6.2 us)
Async XLA Ops:
  7.2 52.8 %copy-start = (bf16[1,704,1408]{2,1,0:T(8,128)(2,1)S(1)}, bf16[1,704,1408]{2,1,0:T(8,128)(2,1)}, u32[]{:S(2)}) copy-start(bf16[1,704,1408]{2,1,0:T(8,128)(2,1)} %param.8) | copy-start | bytes 5947396
  7.2 126.6 %all-gather.5.cloned.1.call-start = ((), (), s32[]{:S(2)}) async-start(), calls=%async_computation.6 | async-start | bytes 5947392 | tf_op jit(solution)/shard_map/all_gather | solution.py:69
  59.0 151.9 %all-gather.3.cloned.1.call-start = ((), (), s32[]{:S(2)}) async-start(), calls=%async_computation.5 | async-start | bytes 5947392 | tf_op jit(solution)/shard_map/all_gather | solution.py:70
  59.8 364.2 %reduce-scatter.4.cloned.1.call-start = ((), (), s32[]{:S(2)}) async-start(), calls=%async_computation.7 | async-start | bytes 11894784
  210.9 11.0 %copy-start.5 = (bf16[128,704]{0,1:T(8,128)(2,1)S(1)}, bf16[128,704]{0,1:T(8,128)(2,1)}, u32[]{:S(2)}) copy-start(bf16[128,704]{0,1:T(8,128)(2,1)} %fusion.31) | copy-start | bytes 540676
  221.9 12.5 %copy-start.4 = (bf16[128,704]{0,1:T(8,128)(2,1)S(1)}, bf16[128,704]{0,1:T(8,128)(2,1)}, u32[]{:S(2)}) copy-start(bf16[128,704]{0,1:T(8,128)(2,1)} %get-tuple-element.9) | copy-start | bytes 540676
  425.8 4.5 copy-start.3
  430.3 0.9 copy-start.1
  431.2 0.9 copy-start.2
  450.2 14.4 %all-to-all-start.3 = ((bf16[8,16,1408]{2,1,0:T(8,128)(2,1)}), bf16[8,16,1408]{2,1,0:T(8,128)(2,1)S(1)}, u32[]{:S(2)}, u32[]{:S(2)}) async-start(bf16[8,16,1408]{2,1,0:T(8,128)(2,1)} %rev.8), calls=%async_computation.3 | async-start | bytes 720896 | tf_op jit(solution)/shard_map/all_to_all | solution.py:34
Sparse Core Ops, SparseCore 0:
  59.1 74.6 all-gather.4
  135.6 75.2 all-gather.2
  259.7 164.1 reduce-scatter.3
where the time goes:
time: 478 us; the launch traced here: 477 us
  waiting for transfers between devices  292 us (61%)
  matrix products  73.5 us (15%)
  blocking collectives  57.8 us (12%)
  local copies, waits for them, and re-layouts  20.4 us (4%)
  other arithmetic  14.1 us (3%)
  between operations  13.8 us (3%)
  starting transfers between devices  5.1 us (1%)
    unnamed x4, waiting for transfers between devices  156 us
    all_gather x1, waiting for transfers between devices, body(): lax.all_gather(key_local, 'seq', axis=0, tiled=True)  71.4 us
    all_gather x1, waiting for transfers between devices, body(): lax.all_gather(value_local, 'seq', axis=0, tiled=True)  56.8 us
    all_to_all x1, blocking collectives, mirror_skip(): lax.all_to_all(pieces, 'section', split_axis=0, concat_axis=0, tiled=True)  22.2 us
    all_to_all x1, blocking collectives, mirror_skip(): lax.all_to_all(jnp.flip(spread, 0), 'section', split_axis=0, concat_axis=...  18.3 us
    unnamed x14, local copies, waits for them, and re-layouts  18 us
    all_to_all x1, blocking collectives, mirror_grad(): lax.all_to_all(pieces, 'section', split_axis=0, concat_axis=0, tiled=True)  17.2 us
    dot_general x1, matrix products, body(): jnp.einsum('rhd,lhd->hrl', grad_heads, gathered_values, preferred_element...  12.5 us
  transfers between devices with their start and end apart: 4, of which 4 were waited for; matrix products, arithmetic and copies ran while one was open for 7% of the time, Pallas kernels for 0%

commit v1 on v0

v1 whole, which is shorter than its diff:
```python
import functools
import math

import jax
import jax.numpy as jnp
from jax import lax
from jax.experimental import pallas as pl
from jax.experimental.pallas import tpu as pltpu
from jax.sharding import PartitionSpec as P

HEADS = 8
EPSILON = 1e-06
CORES = 2
CHUNK = 128
PAD = 8

MESH = pl.DeviceIdType.MESH
F32 = jnp.float32
BF16 = jnp.bfloat16

GRAD, KV, QUERY, OUT, DKV, DQ = range(6)


def dot(a, b):
    return jnp.dot(a, b, preferred_element_type=F32)


def spans(extent, width):
    return [(at, min(width, extent - at)) for at in range(0, extent, width)]


def stats(value):
    center = value - jnp.mean(value, -1, keepdims=True)
    rate = lax.rsqrt(jnp.mean(center * center, -1, keepdims=True) + EPSILON)
    return center * rate, rate


def norm_back(hat, rate, grad):
    inner = jnp.mean(grad * hat, -1, keepdims=True)
    return rate * (grad - jnp.mean(grad, -1, keepdims=True) - hat * inner)


def kernel(
    rows_z,
    rows_x,
    lat_hbm,
    skipw_hbm,
    win_hbm,
    wout_hbm,
    ups_hbm,
    out_hbm,
    glat_hbm,
    lat,
    skipw,
    win,
    wout,
    ups,
    skip_send,
    skip_recv,
    mixed,
    binput,
    normed,
    flip,
    projt,
    gsend,
    kvsend,
    qsend,
    gt,
    qt,
    kv,
    knat,
    vnat,
    qnat,
    gnat,
    exps,
    tops,
    facs,
    delta,
    oacc,
    qacc,
    kvacc,
    ot,
    dqt,
    dkvpart,
    dkvrecv,
    dkvown,
    ofin,
    dqfin,
    dkvfin,
    gpt,
    gnt,
    ginput,
    gm_send,
    gm_recv,
    outv,
    load_sem,
    store_sem,
    col_send,
    col_recv,
    kvx_send,
    kvx_recv,
    dkvx_send,
    dkvx_recv,
    skip_ssem,
    skip_rsem,
    gm_ssem,
    gm_rsem,
):
    sections = lax.axis_size("section")
    section = lax.axis_index("section")
    place = lax.axis_index("seq")
    zl = place // (rows_x * CORES)
    x = lax.rem(place // CORES, rows_x)
    core = lax.rem(place, CORES)
    is_upper = section >= sections // 2
    is_lower = jnp.logical_not(is_upper)
    column = rows_z * CORES
    me = zl * CORES + core

    tok, width = lat.shape
    head_width = wout.shape[0]
    depth = head_width // column
    padded = depth + PAD
    span = column * CHUNK
    scale = 1.0 / math.sqrt(depth)
    rate2 = scale * math.log2(math.e)
    q_tile = 256

    def col_dev(index):
        return {
            "section": section,
            "seq": ((index // CORES) * rows_x + x) * CORES + lax.rem(index, CORES),
        }

    def x_dev(offset):
        there = lax.rem(x + offset + rows_x, rows_x)
        return {"section": section, "seq": (zl * rows_x + there) * CORES + core}

    partner = {"section": sections - 1 - section, "seq": place}

    def remote(src, dst, send, recv, device):
        return pltpu.make_async_remote_copy(
            src_ref=src,
            dst_ref=dst,
            send_sem=send,
            recv_sem=recv,
            device_id=device,
            device_id_type=MESH,
        )

    def lanes(index):
        return pl.ds(pl.multiple_of(index * CHUNK, CHUNK), CHUNK)

    def col_copy(kind, step, src, dst):
        there = lax.rem(me + step, column)
        return remote(
            src(there),
            dst(me),
            col_send.at[kind, step],
            col_recv.at[kind, step],
            col_dev(there),
        )

    def col_own(kind, src, dst):
        return pltpu.make_async_copy(src(me), dst(me), col_recv.at[kind, 0])

    def col_start(kind, src, dst):
        col_own(kind, src, dst).start()

        @pl.loop(1, column)
        def _(step):
            col_copy(kind, step, src, dst).start()

    def col_arrived(kind, src, dst):
        col_own(kind, src, dst).wait()

        @pl.loop(1, column)
        def _(step):
            col_copy(kind, step, src, dst).wait_recv()

    def col_sent(kind, src, dst):
        @pl.loop(1, column)
        def _(step):
            col_copy(kind, step, src, dst).wait_send()

    g_pair = (lambda j: gsend.at[j], lambda j: gt.at[:, lanes(j)])
    kv_pair = (lambda j: kvsend.at[j], lambda j: kv.at[0, :, lanes(j)])
    q_pair = (lambda j: qsend.at[j], lambda j: qt.at[:, lanes(j)])
    o_pair = (lambda j: ot.at[:, lanes(j)], lambda j: ofin.at[j])
    dkv_pair = (lambda j: dkvown.at[:, lanes(j)], lambda j: dkvfin.at[j])
    dq_pair = (lambda j: dqt.at[:, lanes(j)], lambda j: dqfin.at[j])

    loads = [
        pltpu.make_async_copy(src, dst, load_sem.at[i])
        for i, (src, dst) in enumerate(
            [
                (lat_hbm, lat),
                (skipw_hbm, skipw),
                (ups_hbm, ups),
                (wout_hbm, wout),
                (win_hbm, win),
            ]
        )
    ]
    for load in loads:
        load.start()

    barrier = pltpu.get_barrier_semaphore()
    peers = [col_dev(lax.rem(me + step, column)) for step in range(1, column)]
    peers += [x_dev(offset) for offset in range(1, rows_x)]
    peers.append(partner)
    for peer in peers:
        pl.semaphore_signal(barrier, inc=1, device_id=peer, device_id_type=MESH)

    skip_spans = spans(width, 512)

    def skip_copy(i):
        at, size = skip_spans[i]
        cols = pl.ds(at, size)
        return remote(
            skip_send.at[:, cols],
            skip_recv.at[:, cols],
            skip_ssem.at[i],
            skip_rsem.at[i],
            partner,
        )

    loads[0].wait()
    loads[1].wait()
    for i, (at, size) in enumerate(skip_spans):
        product = dot(lat[...], skipw[:, pl.ds(at, size)])
        mixed[:, pl.ds(at, size)] = product
        skip_send[:, pl.ds(at, size)] = product.astype(BF16)
        if i == 0:
            pl.semaphore_wait(barrier, len(peers))

        @pl.when(is_lower)
        def _():
            skip_copy(i).start()

    def turn(source, i):
        block = source[:, pl.ds(i * CHUNK, CHUNK)]
        flip[pl.ds(i * CHUNK, CHUNK), :] = block.astype(F32).T.astype(BF16)

    loads[2].wait()
    for i in range(width // CHUNK):
        turn(ups, i)
    loads[3].wait()
    blank = jnp.zeros((PAD, CHUNK), F32)

    @pl.loop(0, column // 2)
    def _(i):
        rows = pl.ds(pl.multiple_of(i * 2 * depth, 16), 2 * depth)
        pair = dot(wout[rows, :], flip[...])
        gsend[2 * i] = jnp.concatenate([blank, pair[:depth]], 0).astype(BF16)
        gsend[2 * i + 1] = jnp.concatenate([blank, pair[depth:]], 0).astype(BF16)

    col_start(GRAD, *g_pair)

    row_spans = spans(tok, 32)

    @pl.when(is_upper)
    def _():
        for i in range(len(skip_spans)):
            skip_copy(i).wait_recv()
        for at, size in row_spans:
            rows = pl.ds(at, size)
            total = mixed[rows, :] + skip_recv[rows, :].astype(F32)
            mixed[rows, :] = total
            binput[rows, :] = stats(total)[0].astype(BF16)

    @pl.when(is_lower)
    def _():
        binput[...] = lat[...]

    for at, size in row_spans:
        rows = pl.ds(at, size)
        normed[rows, :] = stats(binput[rows, :].astype(F32))[0].astype(BF16)

    loads[4].wait()
    step_cols = 256
    full = 3 * head_width // step_cols
    first = head_width // step_cols

    def project(at, size):
        product = dot(normed[...], win[:, pl.ds(at, size)])
        projt[pl.ds(at, size), :] = product.T

    @pl.loop(first, full)
    def _(i):
        project(pl.multiple_of(i * step_cols, step_cols), step_cols)

    if full * step_cols < 3 * head_width:
        project(full * step_cols, 3 * head_width - full * step_cols)
    for head in range(column):
        keys = projt[pl.ds(head_width + head * depth, depth), :]
        values = projt[pl.ds(2 * head_width + head * depth, depth), :]
        kvsend[head] = jnp.concatenate([keys, values], 0).astype(BF16)
    col_start(KV, *kv_pair)

    @pl.loop(0, first)
    def _(i):
        project(pl.multiple_of(i * step_cols, step_cols), step_cols)

    for head in range(column):
        queries = projt[pl.ds(head * depth, depth), :]
        qsend[head] = jnp.concatenate([queries, blank], 0).astype(BF16)
    col_start(QUERY, *q_pair)

    def kvx_copy(offset, step):
        piece = lanes(lax.rem(me + column - step, column))
        return remote(
            kv.at[0, :, piece],
            kv.at[offset, :, piece],
            kvx_send.at[offset - 1, step],
            kvx_recv.at[offset - 1, step],
            x_dev(offset),
        )

    col_own(KV, *kv_pair).wait()
    for offset in range(1, rows_x):
        kvx_copy(offset, 0).start()

    @pl.loop(1, column)
    def _(step):
        col_copy(KV, step, *kv_pair).wait_recv()
        for offset in range(1, rows_x):
            kvx_copy(offset, step).start()

    def natural(block):
        lane = lax.broadcasted_iota(jnp.int32, (q_tile, padded), 1)
        for at, size in spans(span, q_tile):
            cols = pl.ds(at, size)
            keys = kv[block, :padded, cols].astype(F32).T
            values = kv[block, depth - PAD :, cols].astype(F32).T
            knat[block, cols, :] = keys.astype(BF16)
            vnat[block, cols, :] = jnp.where(lane < PAD, 1.0, values).astype(BF16)

    col_arrived(GRAD, *g_pair)
    col_arrived(QUERY, *q_pair)
    for at, size in spans(span, q_tile):
        rows = pl.ds(at, size)
        qnat[rows, :] = qt[:, rows].astype(F32).T.astype(BF16)
        gnat[rows, :] = gt[:, rows].astype(F32).T

    order = [0] + sorted(range(1, rows_x), key=lambda d: min(d, rows_x - d))

    def forward(block, is_first):
        natural(block)

        @pl.loop(0, span // q_tile)
        def _(i):
            rows = pl.ds(pl.multiple_of(i * q_tile, q_tile), q_tile)
            scores = dot(qnat[rows, :], kv[block, :padded, :])
            top = jnp.max(scores, -1, keepdims=True)
            if not is_first:
                before = tops[order[order.index(block) - 1], rows, :]
                top = jnp.maximum(top, before)
            tops[block, rows, :] = top
            lifted = jnp.exp2((scores - top) * rate2).astype(BF16)
            exps[block, rows, :] = lifted
            term = dot(lifted, vnat[block])
            if not is_first:
                term += oacc[rows, :] * jnp.exp2((before - top) * rate2)
            oacc[rows, :] = term

    for n, block in enumerate(order):
        if n > 0:

            @pl.loop(0, column)
            def _(step):
                kvx_copy(block, step).wait_recv()

        forward(block, n == 0)

    for at, size in spans(span, q_tile):
        rows = pl.ds(at, size)
        total = oacc[rows, :]
        inverse = 1.0 / total[:, :1]
        mixed_values = (total * inverse).astype(BF16).astype(F32)
        ot[:, rows] = mixed_values.T.astype(BF16)
        delta[rows, :] = jnp.sum(gnat[rows, :] * mixed_values, -1, keepdims=True)
        last = tops[order[-1], rows, :]
        for block in range(rows_x):
            lift = jnp.exp2((tops[block, rows, :] - last) * rate2)
            facs[block, rows, :] = lift * inverse
        qacc[rows, :] = jnp.zeros((size, padded), F32)
    col_start(OUT, *o_pair)

    def dkvx_copy(offset):
        return remote(
            dkvpart.at[offset - 1],
            dkvrecv.at[offset - 1],
            dkvx_send.at[offset - 1],
            dkvx_recv.at[offset - 1],
            x_dev(-offset),
        )

    def backward(block):
        kvacc[...] = jnp.zeros_like(kvacc)

        @pl.loop(0, span // q_tile)
        def _(i):
            rows = pl.ds(pl.multiple_of(i * q_tile, q_tile), q_tile)
            factor = facs[block, rows, :]
            grads = gnat[rows, :] * factor
            shift = delta[rows, :] * factor
            lifted = exps[block, rows, :]
            back = dot(grads.astype(BF16), kv[block, depth - PAD :, :]) - shift
            gscore = (lifted.astype(F32) * back).astype(BF16)
            qacc[rows, :] += dot(gscore, knat[block])
            kvacc[:padded, :] += dot(qt[:, rows], gscore)
            kvacc[padded:, :] += dot(grads.T.astype(BF16), lifted)

    def joined(at, size):
        cols = pl.ds(at, size)
        keys = kvacc[:padded, cols] * scale
        values = kvacc[padded:, cols]
        middle = keys[depth - PAD :] + values[: 2 * PAD]
        return jnp.concatenate([keys[: depth - PAD], middle, values[2 * PAD :]], 0)

    for block in reversed(order[1:]):
        backward(block)
        for at, size in spans(span, q_tile):
            dkvpart[block - 1, :, pl.ds(at, size)] = joined(at, size).astype(BF16)
        dkvx_copy(block).start()
    backward(0)
    for offset in range(1, rows_x):
        dkvx_copy(offset).wait_recv()
    for at, size in spans(span, q_tile):
        cols = pl.ds(at, size)
        total = joined(at, size)
        for other in range(rows_x - 1):
            total += dkvrecv[other, :, cols].astype(F32)
        dkvown[:, cols] = total.astype(BF16)
    col_start(DKV, *dkv_pair)
    for at, size in spans(span, q_tile):
        rows = pl.ds(at, size)
        dqt[:, rows] = (qacc[rows, :] * scale).T.astype(BF16)
    col_start(DQ, *dq_pair)

    col_arrived(OUT, *o_pair)
    for head in range(column):
        rows = pl.ds(head * depth, depth)
        projt[rows, :] = ofin[head].astype(F32)[PAD:]
    attended = projt[:head_width, :].T.astype(BF16)
    for at, size in spans(width, 512):
        cols = pl.ds(at, size)
        term = dot(attended, wout[:, cols])
        outv[:, cols] = (binput[:, cols].astype(F32) + term).astype(BF16)
    out_store = pltpu.make_async_copy(outv, out_hbm, store_sem.at[0])
    out_store.start()

    col_arrived(DKV, *dkv_pair)
    for head in range(column):
        both = dkvfin[head].astype(F32)
        projt[pl.ds(head_width + head * depth, depth), :] = both[:depth]
        projt[pl.ds(2 * head_width + head * depth, depth), :] = both[depth:]
    col_arrived(DQ, *dq_pair)
    for head in range(column):
        projt[pl.ds(head * depth, depth), :] = dqfin[head].astype(F32)[:depth]
    gpt[...] = projt[...].astype(BF16)
    half = width // 2

    @pl.loop(0, 2)
    def _(i):
        rows = pl.ds(pl.multiple_of(i * half, 16), half)
        gnt[rows, :] = dot(win[rows, :], gpt[...])

    for i in range(width // CHUNK):
        ginput[:, pl.ds(i * CHUNK, CHUNK)] = gnt[pl.ds(i * CHUNK, CHUNK), :].T

    def gm_copy(i):
        rows = pl.ds(*row_spans[i])
        return remote(
            gm_send.at[rows], gm_recv.at[rows], gm_ssem.at[i], gm_rsem.at[i], partner
        )

    for i, (at, size) in enumerate(row_spans):
        rows = pl.ds(at, size)
        hat, rate = stats(binput[rows, :].astype(F32))
        grad = ups[rows, :].astype(F32) + norm_back(hat, rate, ginput[rows, :])
        ginput[rows, :] = grad

        @pl.when(is_upper)
        def _():
            hat, rate = stats(mixed[rows, :])
            gm_send[rows, :] = norm_back(hat, rate, ginput[rows, :]).astype(BF16)
            gm_copy(i).start()

    @pl.when(is_upper)
    def _():
        ginput[...] = jnp.zeros_like(ginput)
        for i in range(width // CHUNK):
            turn(gm_send, i)

    @pl.when(is_lower)
    def _():
        for i in range(len(row_spans)):
            gm_copy(i).wait_recv()
        for i in range(width // CHUNK):
            turn(gm_recv, i)

    @pl.loop(0, 2)
    def _(i):
        rows = pl.ds(pl.multiple_of(i * half, 16), half)
        gnt[rows, :] = dot(skipw[rows, :], flip[...])

    out_store.wait()
    for i in range(width // CHUNK):
        cols = pl.ds(i * CHUNK, CHUNK)
        term = ginput[:, cols] + gnt[pl.ds(i * CHUNK, CHUNK), :].T
        outv[:, cols] = term.astype(BF16)
    glat_store = pltpu.make_async_copy(outv, glat_hbm, store_sem.at[1])
    glat_store.start()

    for kind, pair in (
        (GRAD, g_pair),
        (KV, kv_pair),
        (QUERY, q_pair),
        (OUT, o_pair),
        (DKV, dkv_pair),
        (DQ, dq_pair),
    ):
        col_sent(kind, *pair)
    for offset in range(1, rows_x):

        @pl.loop(0, column)
        def _(step):
            kvx_copy(offset, step).wait_send()

        dkvx_copy(offset).wait_send()

    @pl.when(is_lower)
    def _():
        for i in range(len(skip_spans)):
            skip_copy(i).wait_send()

    @pl.when(is_upper)
    def _():
        for i in range(len(row_spans)):
            gm_copy(i).wait_send()

    glat_store.wait()


def body(rows_z, rows_x, latents, skip_weight, project_in, project_out, upstream):
    tok, width = latents.shape[1:]
    head_width = project_out.shape[1]
    column = rows_z * CORES
    depth = head_width // column
    padded = depth + PAD
    span = column * tok
    n_skip = len(spans(width, 512))
    n_rows = len(spans(tok, 32))
    wide = (tok, width)
    vmem = pltpu.VMEM
    dma = pltpu.SemaphoreType.DMA
    scratch = [
        vmem(wide, BF16),
        vmem((width, width), BF16),
        vmem((width, 3 * head_width), BF16),
        vmem((head_width, width), BF16),
        vmem(wide, BF16),
        vmem(wide, BF16),
        vmem(wide, BF16),
        vmem(wide, F32),
        vmem(wide, BF16),
        vmem(wide, BF16),
        vmem((width, tok), BF16),
        vmem((3 * head_width, tok), F32),
        vmem((column, padded, tok), BF16),
        vmem((column, 2 * depth, tok), BF16),
        vmem((column, padded, tok), BF16),
        vmem((padded, span), BF16),
        vmem((padded, span), BF16),
        vmem((rows_x, 2 * depth, span), BF16),
        vmem((rows_x, span, padded), BF16),
        vmem((rows_x, span, padded), BF16),
        vmem((span, padded), BF16),
        vmem((span, padded), F32),
        vmem((rows_x, span, span), BF16),
        vmem((rows_x, span, 1), F32),
        vmem((rows_x, span, 1), F32),
        vmem((span, 1), F32),
        vmem((span, padded), F32),
        vmem((span, padded), F32),
        vmem((2 * padded, span), F32),
        vmem((padded, span), BF16),
        vmem((padded, span), BF16),
        vmem((rows_x - 1, 2 * depth, span), BF16),
        vmem((rows_x - 1, 2 * depth, span), BF16),
        vmem((2 * depth, span), BF16),
        vmem((column, padded, tok), BF16),
        vmem((column, padded, tok), BF16),
        vmem((column, 2 * depth, tok), BF16),
        vmem((3 * head_width, tok), BF16),
        vmem((width, tok), F32),
        vmem(wide, F32),
        vmem(wide, BF16),
        vmem(wide, BF16),
        vmem(wide, BF16),
        dma((5,)),
        dma((2,)),
        dma((6, column)),
        dma((6, column)),
        dma((rows_x - 1, column)),
        dma((rows_x - 1, column)),
        dma((rows_x - 1,)),
        dma((rows_x - 1,)),
        dma((n_skip,)),
        dma((n_skip,)),
        dma((n_rows,)),
        dma((n_rows,)),
    ]
    out, glat = pl.pallas_call(
        functools.partial(kernel, rows_z, rows_x),
        out_shape=[jax.ShapeDtypeStruct(wide, BF16)] * 2,
        in_specs=[pl.BlockSpec(memory_space=pl.ANY)] * 5,
        out_specs=[pl.BlockSpec(memory_space=pl.ANY)] * 2,
        scratch_shapes=scratch,
        compiler_params=pltpu.CompilerParams(
            collective_id=0, has_side_effects=True, vmem_limit_bytes=56 * 2**20
        ),
    )(latents[0], skip_weight[0], project_in[0], project_out[0], upstream[0])
    return out[None], glat[None]


def solution(mesh):
    rows_z = HEADS // CORES
    rows_x = mesh.shape["seq"] // HEADS
    return jax.shard_map(
        functools.partial(body, rows_z, rows_x),
        mesh=mesh,
        in_specs=(
            P("section", "seq", None),
            P("section", None, None),
            P("section", None, None),
            P("section", None, None),
            P("section", "seq", None),
        ),
        out_specs=(P("section", "seq", None), P("section", "seq", None)),
        check_vma=False,
    )
```

time: 478 us -> 141 us (0.29)
  the two profiles are of different devices: /device:TPU:8 before, /device:TPU:33 now
where the time goes in v1:
time: 141 us; the launch traced here: 140 us
  Pallas kernels  127 us (90%)
  local copies, waits for them, and re-layouts  12.4 us (9%)
    pallas_call x1, Pallas kernels, body(): pl.pallas_call(functools.partial(kernel, rows_z, rows_x), out_shape=[jax....  127 us
    unnamed x3, local copies, waits for them, and re-layouts  12.4 us

profile of v1, /device:TPU:33, one launch (start us, length us, event | category | flops | bytes accessed | tf_op | source)
XLA Modules:
  0.0 140.2 jit_solution(18144232855158789964)
XLA Ops:
  0.6 8.9 %copy.7 = bf16[1,1408,2112]{2,1,0:T(8,128)(2,1)} copy(bf16[1,1408,2112]{1,2,0:T(8,128)(2,1)} %param.7) | data formatting | bytes 11894784 | tf_op args[2]
  9.6 127.1 %shard_map.68 = (bf16[128,1408]{1,0:T(8,128)(2,1)}, bf16[128,1408]{1,0:T(8,128)(2,1)}) custom-call(bf16[128,1408]{1,0:T(8,128)(2,1)} %bitcast.10, bf16[1408,1408]{1,0:T(8,128)(2,1)} %bitcast.8, bf16[1408,2112]{1,0:T(8,128)(2,1)} %bitcast.7, bf16[704,1408]{1,0:T(8,128)(2,1)} %bitcast.9, bf16[128,1408]{1,0:T(8,128)(2,1)} %bitcast.11), custom_call_target="tpu_custom_call" | custom-call | tf_op jit(solution)/shard_map/pallas_call | solution.py:616
  136.7 1.7 %copy.10 = bf16[1,128,1408]{2,1,0:T(8,128)(2,1)} copy(bf16[1,128,1408]{2,1,0:T(8,128)(2,1)} %bitcast.13) | data formatting | bytes 720896
  138.4 1.7 %copy.11 = bf16[1,128,1408]{2,1,0:T(8,128)(2,1)} copy(bf16[1,128,1408]{2,1,0:T(8,128)(2,1)} %bitcast.12) | data formatting | bytes 720896

commit v2 on v1

--- a/solution.py
+++ b/solution.py
@@ -87,7 +87,7 @@
     ofin,
     dqfin,
     dkvfin,
-    gpt,
+    gproj,
     gnt,
     ginput,
     gm_send,
@@ -277,31 +277,24 @@
         rows = pl.ds(at, size)
         normed[rows, :] = stats(binput[rows, :].astype(F32))[0].astype(BF16)
 
+    for i in range(width // CHUNK):
+        turn(normed, i)
     loads[4].wait()
-    step_cols = 256
-    full = 3 * head_width // step_cols
-    first = head_width // step_cols
-
-    def project(at, size):
-        product = dot(normed[...], win[:, pl.ds(at, size)])
-        projt[pl.ds(at, size), :] = product.T
-
-    @pl.loop(first, full)
-    def _(i):
-        project(pl.multiple_of(i * step_cols, step_cols), step_cols)
-
-    if full * step_cols < 3 * head_width:
-        project(full * step_cols, 3 * head_width - full * step_cols)
+
+    def project(part):
+        rows = pl.ds(pl.multiple_of(part * head_width, 16), head_width)
+        projt[rows, :] = dot(win[rows, :], flip[...])
+
+    @pl.loop(1, 3)
+    def _(part):
+        project(part)
+
     for head in range(column):
         keys = projt[pl.ds(head_width + head * depth, depth), :]
         values = projt[pl.ds(2 * head_width + head * depth, depth), :]
         kvsend[head] = jnp.concatenate([keys, values], 0).astype(BF16)
     col_start(KV, *kv_pair)
-
-    @pl.loop(0, first)
-    def _(i):
-        project(pl.multiple_of(i * step_cols, step_cols), step_cols)
-
+    project(0)
     for head in range(column):
         queries = projt[pl.ds(head * depth, depth), :]
         qsend[head] = jnp.concatenate([queries, blank], 0).astype(BF16)
@@ -459,16 +452,14 @@
     col_arrived(DQ, *dq_pair)
     for head in range(column):
         projt[pl.ds(head * depth, depth), :] = dqfin[head].astype(F32)[:depth]
-    gpt[...] = projt[...].astype(BF16)
-    half = width // 2
-
-    @pl.loop(0, 2)
-    def _(i):
-        rows = pl.ds(pl.multiple_of(i * half, 16), half)
-        gnt[rows, :] = dot(win[rows, :], gpt[...])
-
-    for i in range(width // CHUNK):
-        ginput[:, pl.ds(i * CHUNK, CHUNK)] = gnt[pl.ds(i * CHUNK, CHUNK), :].T
+    for part in range(3):
+        gproj[part] = projt[pl.ds(part * head_width, head_width), :].T.astype(BF16)
+    for at, size in spans(width, 512):
+        cols = pl.ds(at, size)
+        ginput[:, cols] = sum(
+            dot(gproj[part], win[pl.ds(part * head_width, head_width), cols])
+            for part in range(3)
+        )
 
     def gm_copy(i):
         rows = pl.ds(*row_spans[i])
@@ -500,6 +491,8 @@
             gm_copy(i).wait_recv()
         for i in range(width // CHUNK):
             turn(gm_recv, i)
+
+    half = width // 2
 
     @pl.loop(0, 2)
     def _(i):
@@ -542,6 +535,24 @@
             gm_copy(i).wait_send()
 
     glat_store.wait()
+
+
+def settle(out, glat, out_hbm, glat_hbm, held, sem):
+    ins = [
+        pltpu.make_async_copy(out, held.at[0], sem.at[0]),
+        pltpu.make_async_copy(glat, held.at[1], sem.at[1]),
+    ]
+    outs = [
+        pltpu.make_async_copy(held.at[0], out_hbm, sem.at[2]),
+        pltpu.make_async_copy(held.at[1], glat_hbm, sem.at[3]),
+    ]
+    for copy in ins:
+        copy.start()
+    for copy, onward in zip(ins, outs):
+        copy.wait()
+        onward.start()
+    for copy in outs:
+        copy.wait()
 
 
 def body(rows_z, rows_x, latents, skip_weight, project_in, project_out, upstream):
@@ -559,7 +570,7 @@
     scratch = [
         vmem(wide, BF16),
         vmem((width, width), BF16),
-        vmem((width, 3 * head_width), BF16),
+        vmem((3 * head_width, width), BF16),
         vmem((head_width, width), BF16),
         vmem(wide, BF16),
         vmem(wide, BF16),
@@ -594,7 +605,7 @@
         vmem((column, padded, tok), BF16),
         vmem((column, padded, tok), BF16),
         vmem((column, 2 * depth, tok), BF16),
-        vmem((3 * head_width, tok), BF16),
+        vmem((3, tok, head_width), BF16),
         vmem((width, tok), F32),
         vmem(wide, F32),
         vmem(wide, BF16),
@@ -622,7 +633,15 @@
         compiler_params=pltpu.CompilerParams(
             collective_id=0, has_side_effects=True, vmem_limit_bytes=56 * 2**20
         ),
-    )(latents[0], skip_weight[0], project_in[0], project_out[0], upstream[0])
+    )(latents[0], skip_weight[0], project_in[0].T, project_out[0], upstream[0])
+    out, glat = pl.pallas_call(
+        settle,
+        out_shape=[jax.ShapeDtypeStruct(wide, BF16)] * 2,
+        in_specs=[pl.BlockSpec(memory_space=pl.ANY)] * 2,
+        out_specs=[pl.BlockSpec(memory_space=pl.ANY)] * 2,
+        scratch_shapes=[vmem((2,) + wide, BF16), dma((4,))],
+        compiler_params=pltpu.CompilerParams(vmem_limit_bytes=56 * 2**20),
+    )(out, glat)
     return out[None], glat[None]
 
 

time: 141 us -> 128 us (0.908)
  local copies, waits for them, and re-layouts: 12.4 us -> 0 us
    unnamed x3 -> x0, local copies, waits for them, and re-layouts: 12.4 us -> none
    pallas_call x0 -> x1, Pallas kernels: none -> 1.87 us  [body(): pl.pallas_call(settle, out_shape=[jax.ShapeDtypeStruct(wide, BF16)] * 2,...]
    pallas_call x1, Pallas kernels: 127 us -> 125 us  [body(): pl.pallas_call(functools.partial(kernel, rows_z, rows_x), out_shape=[jax....]
where the time goes in v2:
time: 128 us
  Pallas kernels  127 us (99%)
    pallas_call x1, Pallas kernels, body(): pl.pallas_call(functools.partial(kernel, rows_z, rows_x), out_shape=[jax....  125 us

profile of v2, /device:TPU:33, one launch (start us, length us, event | category | flops | bytes accessed | tf_op | source)
XLA Modules:
  0.0 127.8 jit_solution(407541523491442654)
XLA Ops:
  0.6 125.3 %shard_map.68 = (bf16[128,1408]{1,0:T(8,128)(2,1)}, bf16[128,1408]{1,0:T(8,128)(2,1)}) custom-call(bf16[128,1408]{1,0:T(8,128)(2,1)} %bitcast.12, bf16[1408,1408]{1,0:T(8,128)(2,1)} %bitcast.10, bf16[2112,1408]{1,0:T(8,128)(2,1)} %bitcast.9, bf16[704,1408]{1,0:T(8,128)(2,1)} %bitcast.11, bf16[128,1408]{1,0:T(8,128)(2,1)} %bitcast.13), custom_call_target="tpu_custom_call" | custom-call | tf_op jit(solution)/shard_map/pallas_call | solution.py:627
  125.9 1.9 %shard_map.69 = (bf16[128,1408]{1,0:T(8,128)(2,1)}, bf16[128,1408]{1,0:T(8,128)(2,1)}) custom-call(bf16[128,1408]{1,0:T(8,128)(2,1)} %get-tuple-element.6.out, bf16[128,1408]{1,0:T(8,128)(2,1)} %get-tuple-element.7.glat), custom_call_target="tpu_custom_call" | custom-call | tf_op jit(solution)/shard_map/pallas_call | solution.py:637

commit v3 on v2

--- a/solution.py
+++ b/solution.py
@@ -18,7 +18,7 @@
 F32 = jnp.float32
 BF16 = jnp.bfloat16
 
-GRAD, KV, QUERY, OUT, DKV, DQ = range(6)
+GRAD, QUERY, OUT, DQ = range(4)
 
 
 def dot(a, b):
@@ -81,6 +81,10 @@
     kvacc,
     ot,
     dqt,
+    kvin,
+    keep,
+    dkvgive,
+    dkvtake,
     dkvpart,
     dkvrecv,
     dkvown,
@@ -97,8 +101,17 @@
     store_sem,
     col_send,
     col_recv,
+    kv_send,
+    kv_recv,
     kvx_send,
     kvx_recv,
+    kvs_send,
+    kvs_recv,
+    place_sem,
+    dkvs_send,
+    dkvs_recv,
+    dkv_send,
+    dkv_recv,
     dkvx_send,
     dkvx_recv,
     skip_ssem,
@@ -115,7 +128,12 @@
     is_upper = section >= sections // 2
     is_lower = jnp.logical_not(is_upper)
     column = rows_z * CORES
+    part_size = column // 2
     me = zl * CORES + core
+    even = lax.rem(x, 2)
+    pair = x // 2
+    own_head = 2 * zl + even
+    query_x = 2 * pair + core
 
     tok, width = lat.shape
     head_width = wout.shape[0]
@@ -126,16 +144,20 @@
     rate2 = scale * math.log2(math.e)
     q_tile = 256
 
-    def col_dev(index):
+    def device(z, at_x, at_core):
         return {
             "section": section,
-            "seq": ((index // CORES) * rows_x + x) * CORES + lax.rem(index, CORES),
+            "seq": (z * rows_x + at_x) * CORES + at_core,
         }
 
-    def x_dev(offset):
-        there = lax.rem(x + offset + rows_x, rows_x)
-        return {"section": section, "seq": (zl * rows_x + there) * CORES + core}
-
+    def owner(index, at_x):
+        return device(index // CORES, at_x, lax.rem(index, CORES))
+
+    def across(offset):
+        there = (x, x + 1 - 2 * even, lax.rem(x + 2, rows_x), rows_x - 1 - x)[offset]
+        return device(zl, there, core)
+
+    sibling = device(zl, x, 1 - core)
     partner = {"section": sections - 1 - section, "seq": place}
 
     def remote(src, dst, send, recv, device):
@@ -151,68 +173,252 @@
     def lanes(index):
         return pl.ds(pl.multiple_of(index * CHUNK, CHUNK), CHUNK)
 
-    def col_copy(kind, step, src, dst):
-        there = lax.rem(me + step, column)
-        return remote(
-            src(there),
-            dst(me),
-            col_send.at[kind, step],
-            col_recv.at[kind, step],
-            col_dev(there),
-        )
-
-    def col_own(kind, src, dst):
-        return pltpu.make_async_copy(src(me), dst(me), col_recv.at[kind, 0])
-
-    def col_start(kind, src, dst):
-        col_own(kind, src, dst).start()
-
-        @pl.loop(1, column)
+    def head_copy(kind, head, src, dst):
+        there = device(head // 2, 2 * pair + lax.rem(head, 2), even)
+        return remote(
+            src.at[head],
+            dst.at[:, lanes(me)],
+            col_send.at[kind, head],
+            col_recv.at[kind, me],
+            there,
+        )
+
+    def back_copy(kind, index, src, dst):
+        return remote(
+            src.at[:, lanes(index)],
+            dst.at[own_head],
+            col_send.at[kind, index],
+            col_recv.at[kind, own_head],
+            owner(index, query_x),
+        )
+
+    def head_start(kind, src, dst):
+        @pl.loop(0, column)
         def _(step):
-            col_copy(kind, step, src, dst).start()
-
-    def col_arrived(kind, src, dst):
-        col_own(kind, src, dst).wait()
-
-        @pl.loop(1, column)
+            head = lax.rem(own_head + step, column)
+            mine = (step == 0) & (even == core)
+
+            @pl.when(mine)
+            def _():
+                pltpu.make_async_copy(
+                    src.at[head], dst.at[:, lanes(me)], col_recv.at[kind, me]
+                ).start()
+
+            @pl.when(jnp.logical_not(mine))
+            def _():
+                head_copy(kind, head, src, dst).start()
+
+    def head_arrived(kind, src, dst):
+        @pl.loop(0, column)
+        def _(index):
+            pltpu.make_async_copy(
+                src.at[0], dst.at[:, lanes(index)], col_recv.at[kind, index]
+            ).wait()
+
+    def head_sent(kind, src, dst):
+        @pl.loop(0, column)
         def _(step):
-            col_copy(kind, step, src, dst).wait_recv()
-
-    def col_sent(kind, src, dst):
-        @pl.loop(1, column)
+            head = lax.rem(own_head + step, column)
+
+            @pl.when((step > 0) | (even != core))
+            def _():
+                head_copy(kind, head, src, dst).wait_send()
+
+    def back_start(kind, src, dst):
+        @pl.loop(0, column)
         def _(step):
-            col_copy(kind, step, src, dst).wait_send()
-
-    g_pair = (lambda j: gsend.at[j], lambda j: gt.at[:, lanes(j)])
-    kv_pair = (lambda j: kvsend.at[j], lambda j: kv.at[0, :, lanes(j)])
-    q_pair = (lambda j: qsend.at[j], lambda j: qt.at[:, lanes(j)])
-    o_pair = (lambda j: ot.at[:, lanes(j)], lambda j: ofin.at[j])
-    dkv_pair = (lambda j: dkvown.at[:, lanes(j)], lambda j: dkvfin.at[j])
-    dq_pair = (lambda j: dqt.at[:, lanes(j)], lambda j: dqfin.at[j])
-
+            index = lax.rem(me + step, column)
+            mine = (step == 0) & (even == core)
+
+            @pl.when(mine)
+            def _():
+                pltpu.make_async_copy(
+                    src.at[:, lanes(index)],
+                    dst.at[own_head],
+                    col_recv.at[kind, own_head],
+                ).start()
+
+            @pl.when(jnp.logical_not(mine))
+            def _():
+                back_copy(kind, index, src, dst).start()
+
+    def back_arrived(kind, src, dst):
+        @pl.loop(0, column)
+        def _(head):
+            pltpu.make_async_copy(
+                src.at[:, lanes(0)], dst.at[head], col_recv.at[kind, head]
+            ).wait()
+
+    def back_sent(kind, src, dst):
+        @pl.loop(0, column)
+        def _(step):
+            index = lax.rem(me + step, column)
+
+            @pl.when((step > 0) | (even != core))
+            def _():
+                back_copy(kind, index, src, dst).wait_send()
+
+    half_core = me // part_size
+    half_at = lax.rem(me, part_size)
+    kv_mine = half_core == core
+
+    def kv_copy(step):
+        z = lax.rem(zl + step, rows_z)
+        return remote(
+            kvsend.at[pl.ds(2 * z, 2)],
+            kvin.at[:, :, lanes(half_at)],
+            kv_send.at[step],
+            kv_recv.at[half_at],
+            device(z, x, half_core),
+        )
+
+    def kv_own():
+        return pltpu.make_async_copy(
+            kvsend.at[pl.ds(2 * zl, 2)],
+            kvin.at[:, :, lanes(half_at)],
+            kv_recv.at[half_at],
+        )
+
+    def kv_start():
+        @pl.when(kv_mine)
+        def _():
+            kv_own().start()
+
+        @pl.when(jnp.logical_not(kv_mine))
+        def _():
+            kv_copy(0).start()
+
+        @pl.loop(1, rows_z)
+        def _(step):
+            kv_copy(step).start()
+
+    def kv_arrived(at):
+        pltpu.make_async_copy(
+            kvsend.at[pl.ds(0, 2)], kvin.at[:, :, lanes(at)], kv_recv.at[at]
+        ).wait()
+
+    def kv_sent():
+        @pl.when(jnp.logical_not(kv_mine))
+        def _():
+            kv_copy(0).wait_send()
+
+        @pl.loop(1, rows_z)
+        def _(step):
+            kv_copy(step).wait_send()
+
+    def half_lanes(at):
+        return lanes(core * part_size + at)
+
+    def kvx_copy(offset, at):
+        head = even if offset == 2 else 1 - even
+        return remote(
+            kvin.at[head, :, lanes(at)],
+            kv.at[offset, :, half_lanes(at)],
+            kvx_send.at[offset - 1, at],
+            kvx_recv.at[offset - 1, at],
+            across(offset),
+        )
+
+    def kvs_copy(offset, at):
+        there = kv.at[offset, :, half_lanes(at)]
+        here = kvin.at[even, :, lanes(at)] if offset == 0 else there
+        return remote(
+            here, there, kvs_send.at[offset, at], kvs_recv.at[offset, at], sibling
+        )
+
+    def kv_place(at):
+        return pltpu.make_async_copy(
+            kvin.at[even, :, lanes(at)], kv.at[0, :, half_lanes(at)], place_sem.at[at]
+        )
+
+    def dkvs_copy(block):
+        return remote(
+            dkvgive.at[block],
+            dkvtake.at[block],
+            dkvs_send.at[block],
+            dkvs_recv.at[block],
+            sibling,
+        )
+
+    def dkvx_copy(offset):
+        return remote(
+            dkvpart.at[offset - 1],
+            dkvrecv.at[offset - 1],
+            dkvx_send.at[offset - 1],
+            dkvx_recv.at[offset - 1],
+            across(offset),
+        )
+
+    def dkv_copy(which, at):
+        head = 2 * zl + (even if which == 0 else 1 - even)
+        return remote(
+            dkvown.at[which, :, lanes(at)],
+            dkvfin.at[head],
+            dkv_send.at[which, at],
+            dkv_recv.at[head],
+            owner(core * part_size + at, x),
+        )
+
+    def dkv_start(which):
+        head = 2 * zl + (even if which == 0 else 1 - even)
+
+        @pl.loop(0, part_size)
+        def _(step):
+            at = lax.rem(half_at + step, part_size)
+            mine = (step == 0) & kv_mine
+
+            @pl.when(mine)
+            def _():
+                pltpu.make_async_copy(
+                    dkvown.at[which, :, lanes(at)], dkvfin.at[head], dkv_recv.at[head]
+                ).start()
+
+            @pl.when(jnp.logical_not(mine))
+            def _():
+                dkv_copy(which, at).start()
+
+    def dkv_sent(which):
+        @pl.loop(0, part_size)
+        def _(step):
+            at = lax.rem(half_at + step, part_size)
+
+            @pl.when((step > 0) | jnp.logical_not(kv_mine))
+            def _():
+                dkv_copy(which, at).wait_send()
+
+    def dkv_arrived():
+        @pl.loop(0, column)
+        def _(head):
+            pltpu.make_async_copy(
+                dkvown.at[0, :, lanes(0)], dkvfin.at[head], dkv_recv.at[head]
+            ).wait()
+
+    g_pair = (gsend, gt)
+    q_pair = (qsend, qt)
+    o_pair = (ot, ofin)
+    dq_pair = (dqt, dqfin)
+
+    skip_spans = spans(width, 512)
+    pieces = [(lat_hbm, lat)]
+    for at, size in skip_spans:
+        cols = pl.ds(at, size)
+        pieces.append((skipw_hbm.at[:, cols], skipw.at[:, cols]))
+    pieces += [(ups_hbm, ups), (wout_hbm, wout), (win_hbm, win)]
     loads = [
         pltpu.make_async_copy(src, dst, load_sem.at[i])
-        for i, (src, dst) in enumerate(
-            [
-                (lat_hbm, lat),
-                (skipw_hbm, skipw),
-                (ups_hbm, ups),
-                (wout_hbm, wout),
-                (win_hbm, win),
-            ]
-        )
+        for i, (src, dst) in enumerate(pieces)
     ]
+    lat_load, *skip_loads, ups_load, wout_load, win_load = loads
     for load in loads:
         load.start()
 
     barrier = pltpu.get_barrier_semaphore()
-    peers = [col_dev(lax.rem(me + step, column)) for step in range(1, column)]
-    peers += [x_dev(offset) for offset in range(1, rows_x)]
+    peers = [owner(lax.rem(me + step, column), x) for step in range(1, column)]
+    peers += [owner(index, x + 1 - 2 * even) for index in range(column)]
+    peers += [across(offset) for offset in range(2, rows_x)]
     peers.append(partner)
     for peer in peers:
         pl.semaphore_signal(barrier, inc=1, device_id=peer, device_id_type=MESH)
-
-    skip_spans = spans(width, 512)
 
     def skip_copy(i):
         at, size = skip_spans[i]
@@ -225,9 +431,9 @@
             partner,
         )
 
-    loads[0].wait()
-    loads[1].wait()
+    lat_load.wait()
     for i, (at, size) in enumerate(skip_spans):
+        skip_loads[i].wait()
         product = dot(lat[...], skipw[:, pl.ds(at, size)])
         mixed[:, pl.ds(at, size)] = product
         skip_send[:, pl.ds(at, size)] = product.astype(BF16)
@@ -242,20 +448,20 @@
         block = source[:, pl.ds(i * CHUNK, CHUNK)]
         flip[pl.ds(i * CHUNK, CHUNK), :] = block.astype(F32).T.astype(BF16)
 
-    loads[2].wait()
+    ups_load.wait()
     for i in range(width // CHUNK):
         turn(ups, i)
-    loads[3].wait()
+    wout_load.wait()
     blank = jnp.zeros((PAD, CHUNK), F32)
 
     @pl.loop(0, column // 2)
     def _(i):
         rows = pl.ds(pl.multiple_of(i * 2 * depth, 16), 2 * depth)
-        pair = dot(wout[rows, :], flip[...])
-        gsend[2 * i] = jnp.concatenate([blank, pair[:depth]], 0).astype(BF16)
-        gsend[2 * i + 1] = jnp.concatenate([blank, pair[depth:]], 0).astype(BF16)
-
-    col_start(GRAD, *g_pair)
+        two = dot(wout[rows, :], flip[...])
+        gsend[2 * i] = jnp.concatenate([blank, two[:depth]], 0).astype(BF16)
+        gsend[2 * i + 1] = jnp.concatenate([blank, two[depth:]], 0).astype(BF16)
+
+    head_start(GRAD, *g_pair)
 
     row_spans = spans(tok, 32)
 
@@ -279,7 +485,7 @@
 
     for i in range(width // CHUNK):
         turn(normed, i)
-    loads[4].wait()
+    win_load.wait()
 
     def project(part):
         rows = pl.ds(pl.multiple_of(part * head_width, 16), head_width)
@@ -293,32 +499,26 @@
         keys = projt[pl.ds(head_width + head * depth, depth), :]
         values = projt[pl.ds(2 * head_width + head * depth, depth), :]
         kvsend[head] = jnp.concatenate([keys, values], 0).astype(BF16)
-    col_start(KV, *kv_pair)
+    kv_start()
     project(0)
     for head in range(column):
         queries = projt[pl.ds(head * depth, depth), :]
         qsend[head] = jnp.concatenate([queries, blank], 0).astype(BF16)
-    col_start(QUERY, *q_pair)
-
-    def kvx_copy(offset, step):
-        piece = lanes(lax.rem(me + column - step, column))
-        return remote(
-            kv.at[0, :, piece],
-            kv.at[offset, :, piece],
-            kvx_send.at[offset - 1, step],
-            kvx_recv.at[offset - 1, step],
-            x_dev(offset),
-        )
-
-    col_own(KV, *kv_pair).wait()
-    for offset in range(1, rows_x):
-        kvx_copy(offset, 0).start()
-
-    @pl.loop(1, column)
-    def _(step):
-        col_copy(KV, step, *kv_pair).wait_recv()
+    head_start(QUERY, *q_pair)
+
+    @pl.loop(0, part_size)
+    def _(at):
+        kv_arrived(at)
         for offset in range(1, rows_x):
-            kvx_copy(offset, step).start()
+            kvx_copy(offset, at).start()
+        kvs_copy(0, at).start()
+        kv_place(at).start()
+
+    @pl.loop(0, part_size)
+    def _(at):
+        for offset in range(1, rows_x):
+            kvx_copy(offset, at).wait_recv()
+            kvs_copy(offset, at).start()
 
     def natural(block):
         lane = lax.broadcasted_iota(jnp.int32, (q_tile, padded), 1)
@@ -329,14 +529,14 @@
             knat[block, cols, :] = keys.astype(BF16)
             vnat[block, cols, :] = jnp.where(lane < PAD, 1.0, values).astype(BF16)
 
-    col_arrived(GRAD, *g_pair)
-    col_arrived(QUERY, *q_pair)
+    head_arrived(GRAD, *g_pair)
+    head_arrived(QUERY, *q_pair)
     for at, size in spans(span, q_tile):
         rows = pl.ds(at, size)
         qnat[rows, :] = qt[:, rows].astype(F32).T.astype(BF16)
         gnat[rows, :] = gt[:, rows].astype(F32).T
 
-    order = [0] + sorted(range(1, rows_x), key=lambda d: min(d, rows_x - d))
+    order = [0, 1, 3, 2]
 
     def forward(block, is_first):
         natural(block)
@@ -358,11 +558,12 @@
             oacc[rows, :] = term
 
     for n, block in enumerate(order):
-        if n > 0:
-
-            @pl.loop(0, column)
-            def _(step):
-                kvx_copy(block, step).wait_recv()
+
+        @pl.loop(0, part_size)
+        def _(at):
+            kvs_copy(block, at).wait_recv()
+            if block == 0:
+                kv_place(at).wait()
 
         forward(block, n == 0)
 
@@ -378,61 +579,65 @@
             lift = jnp.exp2((tops[block, rows, :] - last) * rate2)
             facs[block, rows, :] = lift * inverse
         qacc[rows, :] = jnp.zeros((size, padded), F32)
-    col_start(OUT, *o_pair)
-
-    def dkvx_copy(offset):
-        return remote(
-            dkvpart.at[offset - 1],
-            dkvrecv.at[offset - 1],
-            dkvx_send.at[offset - 1],
-            dkvx_recv.at[offset - 1],
-            x_dev(-offset),
-        )
-
-    def backward(block):
-        kvacc[...] = jnp.zeros_like(kvacc)
-
-        @pl.loop(0, span // q_tile)
-        def _(i):
-            rows = pl.ds(pl.multiple_of(i * q_tile, q_tile), q_tile)
-            factor = facs[block, rows, :]
-            grads = gnat[rows, :] * factor
-            shift = delta[rows, :] * factor
-            lifted = exps[block, rows, :]
-            back = dot(grads.astype(BF16), kv[block, depth - PAD :, :]) - shift
-            gscore = (lifted.astype(F32) * back).astype(BF16)
-            qacc[rows, :] += dot(gscore, knat[block])
-            kvacc[:padded, :] += dot(qt[:, rows], gscore)
-            kvacc[padded:, :] += dot(grads.T.astype(BF16), lifted)
-
-    def joined(at, size):
-        cols = pl.ds(at, size)
+    back_start(OUT, *o_pair)
+
+    def backward_rows(block, i):
+        rows = pl.ds(i * q_tile, q_tile)
+        factor = facs[block, rows, :]
+        grads = gnat[rows, :] * factor
+        shift = delta[rows, :] * factor
+        lifted = exps[block, rows, :]
+        back = dot(grads.astype(BF16), kv[block, depth - PAD :, :]) - shift
+        gscore = (lifted.astype(F32) * back).astype(BF16)
+        qacc[rows, :] += dot(gscore, knat[block])
+        keys = dot(qt[:, rows], gscore)
+        values = dot(grads.T.astype(BF16), lifted)
+        if i > 0:
+            keys += kvacc[:padded, :]
+            values += kvacc[padded:, :]
+        kvacc[:padded, :] = keys
+        kvacc[padded:, :] = values
+
+    half_span = span // 2
+
+    def joined(which):
+        cols = pl.ds(pl.multiple_of(which * half_span, CHUNK), half_span)
         keys = kvacc[:padded, cols] * scale
         values = kvacc[padded:, cols]
         middle = keys[depth - PAD :] + values[: 2 * PAD]
         return jnp.concatenate([keys[: depth - PAD], middle, values[2 * PAD :]], 0)
 
-    for block in reversed(order[1:]):
-        backward(block)
-        for at, size in spans(span, q_tile):
-            dkvpart[block - 1, :, pl.ds(at, size)] = joined(at, size).astype(BF16)
+    def pass_on(block):
+        dkvs_copy(block).wait_recv()
+        total = keep[block] + dkvtake[block].astype(F32)
+        dkvpart[block - 1] = total.astype(BF16)
         dkvx_copy(block).start()
-    backward(0)
-    for offset in range(1, rows_x):
+
+    turns = [2, 1, 3, 0]
+    for n, block in enumerate(turns):
+        for i in range(span // q_tile):
+            backward_rows(block, i)
+            if n > 0 and i == (span // q_tile - 1) // 2:
+                pass_on(turns[n - 1])
+        dkvgive[block] = joined(1 - core).astype(BF16)
+        dkvs_copy(block).start()
+        keep[block] = joined(core)
+
+    for offset in (1, 3):
         dkvx_copy(offset).wait_recv()
-    for at, size in spans(span, q_tile):
-        cols = pl.ds(at, size)
-        total = joined(at, size)
-        for other in range(rows_x - 1):
-            total += dkvrecv[other, :, cols].astype(F32)
-        dkvown[:, cols] = total.astype(BF16)
-    col_start(DKV, *dkv_pair)
+    dkvown[1] = (dkvrecv[0].astype(F32) + dkvrecv[2].astype(F32)).astype(BF16)
+    dkv_start(1)
+    dkvs_copy(0).wait_recv()
+    dkvx_copy(2).wait_recv()
+    total = keep[0] + dkvtake[0].astype(F32) + dkvrecv[1].astype(F32)
+    dkvown[0] = total.astype(BF16)
+    dkv_start(0)
     for at, size in spans(span, q_tile):
         rows = pl.ds(at, size)
         dqt[:, rows] = (qacc[rows, :] * scale).T.astype(BF16)
-    col_start(DQ, *dq_pair)
-
-    col_arrived(OUT, *o_pair)
+    back_start(DQ, *dq_pair)
+
+    back_arrived(OUT, *o_pair)
     for head in range(column):
         rows = pl.ds(head * depth, depth)
         projt[rows, :] = ofin[head].astype(F32)[PAD:]
@@ -444,12 +649,12 @@
     out_store = pltpu.make_async_copy(outv, out_hbm, store_sem.at[0])
     out_store.start()
 
-    col_arrived(DKV, *dkv_pair)
+    dkv_arrived()
     for head in range(column):
         both = dkvfin[head].astype(F32)
         projt[pl.ds(head_width + head * depth, depth), :] = both[:depth]
         projt[pl.ds(2 * head_width + head * depth, depth), :] = both[depth:]
-    col_arrived(DQ, *dq_pair)
+    back_arrived(DQ, *dq_pair)
     for head in range(column):
         projt[pl.ds(head * depth, depth), :] = dqfin[head].astype(F32)[:depth]
     for part in range(3):
@@ -507,22 +712,25 @@
     glat_store = pltpu.make_async_copy(outv, glat_hbm, store_sem.at[1])
     glat_store.start()
 
-    for kind, pair in (
-        (GRAD, g_pair),
-        (KV, kv_pair),
-        (QUERY, q_pair),
-        (OUT, o_pair),
-        (DKV, dkv_pair),
-        (DQ, dq_pair),
-    ):
-        col_sent(kind, *pair)
+    head_sent(GRAD, *g_pair)
+    head_sent(QUERY, *q_pair)
+    back_sent(OUT, *o_pair)
+    back_sent(DQ, *dq_pair)
+    kv_sent()
+    dkv_sent(0)
+    dkv_sent(1)
+
+    @pl.loop(0, part_size)
+    def _(at):
+        kvs_copy(0, at).wait_send()
+        for offset in range(1, rows_x):
+            kvx_copy(offset, at).wait_send()
+            kvs_copy(offset, at).wait_send()
+
+    dkvs_copy(0).wait_send()
     for offset in range(1, rows_x):
-
-        @pl.loop(0, column)
-        def _(step):
-            kvx_copy(offset, step).wait_send()
-
         dkvx_copy(offset).wait_send()
+        dkvs_copy(offset).wait_send()
 
     @pl.when(is_lower)
     def _():
@@ -562,6 +770,7 @@
     depth = head_width // column
     padded = depth + PAD
     span = column * tok
+    part = span // 2
     n_skip = len(spans(width, 512))
     n_rows = len(spans(tok, 32))
     wide = (tok, width)
@@ -599,9 +808,13 @@
         vmem((2 * padded, span), F32),
         vmem((padded, span), BF16),
         vmem((padded, span), BF16),
-        vmem((rows_x - 1, 2 * depth, span), BF16),
-        vmem((rows_x - 1, 2 * depth, span), BF16),
-        vmem((2 * depth, span), BF16),
+        vmem((2, 2 * depth, part), BF16),
+        vmem((rows_x, 2 * depth, part), F32),
+        vmem((rows_x, 2 * depth, part), BF16),
+        vmem((rows_x, 2 * depth, part), BF16),
+        vmem((rows_x - 1, 2 * depth, part), BF16),
+        vmem((rows_x - 1, 2 * depth, part), BF16),
+        vmem((2, 2 * depth, part), BF16),
         vmem((column, padded, tok), BF16),
         vmem((column, padded, tok), BF16),
         vmem((column, 2 * depth, tok), BF16),
@@ -611,12 +824,21 @@
         vmem(wide, BF16),
         vmem(wide, BF16),
         vmem(wide, BF16),
-        dma((5,)),
+        dma((4 + n_skip,)),
         dma((2,)),
-        dma((6, column)),
-        dma((6, column)),
-        dma((rows_x - 1, column)),
-        dma((rows_x - 1, column)),
+        dma((4, column)),
+        dma((4, column)),
+        dma((rows_z,)),
+        dma((column // 2,)),
+        dma((rows_x - 1, column // 2)),
+        dma((rows_x - 1, column // 2)),
+        dma((rows_x, column // 2)),
+        dma((rows_x, column // 2)),
+        dma((column // 2,)),
+        dma((rows_x,)),
+        dma((rows_x,)),
+        dma((2, column // 2)),
+        dma((column,)),
         dma((rows_x - 1,)),
         dma((rows_x - 1,)),
         dma((n_skip,)),

time: 128 us -> 122 us (0.953)
  Pallas kernels: 127 us -> 121 us
    pallas_call x1, Pallas kernels: 125 us -> 119 us  [body(): pl.pallas_call(functools.partial(kernel, rows_z, rows_x), out_shape=[jax....]
where the time goes in v3:
time: 122 us
  Pallas kernels  121 us (99%)
    pallas_call x1, Pallas kernels, body(): pl.pallas_call(functools.partial(kernel, rows_z, rows_x), out_shape=[jax....  119 us

profile of v3, /device:TPU:33, one launch (start us, length us, event | category | flops | bytes accessed | tf_op | source)
XLA Modules:
  0.0 121.6 jit_solution(11700991833586464660)
XLA Ops:
  0.6 118.9 %shard_map.68 = (bf16[128,1408]{1,0:T(8,128)(2,1)}, bf16[128,1408]{1,0:T(8,128)(2,1)}) custom-call(bf16[128,1408]{1,0:T(8,128)(2,1)} %bitcast.12, bf16[1408,1408]{1,0:T(8,128)(2,1)} %bitcast.10, bf16[2112,1408]{1,0:T(8,128)(2,1)} %bitcast.9, bf16[704,1408]{1,0:T(8,128)(2,1)} %bitcast.11, bf16[128,1408]{1,0:T(8,128)(2,1)} %bitcast.13), custom_call_target="tpu_custom_call" | custom-call | tf_op jit(solution)/shard_map/pallas_call | solution.py:849
  119.5 1.9 %shard_map.69 = (bf16[128,1408]{1,0:T(8,128)(2,1)}, bf16[128,1408]{1,0:T(8,128)(2,1)}) custom-call(bf16[128,1408]{1,0:T(8,128)(2,1)} %get-tuple-element.6.out, bf16[128,1408]{1,0:T(8,128)(2,1)} %get-tuple-element.7.glat), custom_call_target="tpu_custom_call" | custom-call | tf_op jit(solution)/shard_map/pallas_call | solution.py:859

commit v4 on v3

--- a/solution.py
+++ b/solution.py
@@ -41,8 +41,8 @@
 
 
 def kernel(
-    rows_z,
-    rows_x,
+    rows_h,
+    rows_k,
     lat_hbm,
     skipw_hbm,
     win_hbm,
@@ -122,18 +122,18 @@
     sections = lax.axis_size("section")
     section = lax.axis_index("section")
     place = lax.axis_index("seq")
-    zl = place // (rows_x * CORES)
-    x = lax.rem(place // CORES, rows_x)
+    line = place // (rows_h * CORES)
+    row = lax.rem(place // CORES, rows_h)
     core = lax.rem(place, CORES)
     is_upper = section >= sections // 2
     is_lower = jnp.logical_not(is_upper)
-    column = rows_z * CORES
+    column = rows_h * CORES
     part_size = column // 2
-    me = zl * CORES + core
-    even = lax.rem(x, 2)
-    pair = x // 2
-    own_head = 2 * zl + even
-    query_x = 2 * pair + core
+    me = row * CORES + core
+    even = lax.rem(line, 2)
+    pair = line // 2
+    own_head = 2 * row + even
+    query_line = 2 * pair + core
 
     tok, width = lat.shape
     head_width = wout.shape[0]
@@ -144,20 +144,20 @@
     rate2 = scale * math.log2(math.e)
     q_tile = 256
 
-    def device(z, at_x, at_core):
+    def device(at_row, at_line, at_core):
         return {
             "section": section,
-            "seq": (z * rows_x + at_x) * CORES + at_core,
+            "seq": (at_line * rows_h + at_row) * CORES + at_core,
         }
 
-    def owner(index, at_x):
-        return device(index // CORES, at_x, lax.rem(index, CORES))
+    def owner(index, at_line):
+        return device(index // CORES, at_line, lax.rem(index, CORES))
 
     def across(offset):
-        there = (x, x + 1 - 2 * even, lax.rem(x + 2, rows_x), rows_x - 1 - x)[offset]
-        return device(zl, there, core)
-
-    sibling = device(zl, x, 1 - core)
+        there = (line, line + 1 - 2 * even, lax.rem(line + 2, rows_k), rows_k - 1 - line)[offset]
+        return device(row, there, core)
+
+    sibling = device(row, line, 1 - core)
     partner = {"section": sections - 1 - section, "seq": place}
 
     def remote(src, dst, send, recv, device):
@@ -189,7 +189,7 @@
             dst.at[own_head],
             col_send.at[kind, index],
             col_recv.at[kind, own_head],
-            owner(index, query_x),
+            owner(index, query_line),
         )
 
     def head_start(kind, src, dst):
@@ -224,23 +224,23 @@
             def _():
                 head_copy(kind, head, src, dst).wait_send()
 
+    def back_one(kind, index, src, dst):
+        mine = (index == me) & (even == core)
+
+        @pl.when(mine)
+        def _():
+            pltpu.make_async_copy(
+                src.at[:, lanes(index)], dst.at[own_head], col_recv.at[kind, own_head]
+            ).start()
+
+        @pl.when(jnp.logical_not(mine))
+        def _():
+            back_copy(kind, index, src, dst).start()
+
     def back_start(kind, src, dst):
         @pl.loop(0, column)
-        def _(step):
-            index = lax.rem(me + step, column)
-            mine = (step == 0) & (even == core)
-
-            @pl.when(mine)
-            def _():
-                pltpu.make_async_copy(
-                    src.at[:, lanes(index)],
-                    dst.at[own_head],
-                    col_recv.at[kind, own_head],
-                ).start()
-
-            @pl.when(jnp.logical_not(mine))
-            def _():
-                back_copy(kind, index, src, dst).start()
+        def _(index):
+            back_one(kind, index, src, dst)
 
     def back_arrived(kind, src, dst):
         @pl.loop(0, column)
@@ -263,18 +263,18 @@
     kv_mine = half_core == core
 
     def kv_copy(step):
-        z = lax.rem(zl + step, rows_z)
+        at_row = lax.rem(row + step, rows_h)
         return remote(
-            kvsend.at[pl.ds(2 * z, 2)],
+            kvsend.at[pl.ds(2 * at_row, 2)],
             kvin.at[:, :, lanes(half_at)],
             kv_send.at[step],
             kv_recv.at[half_at],
-            device(z, x, half_core),
+            device(at_row, line, half_core),
         )
 
     def kv_own():
         return pltpu.make_async_copy(
-            kvsend.at[pl.ds(2 * zl, 2)],
+            kvsend.at[pl.ds(2 * row, 2)],
             kvin.at[:, :, lanes(half_at)],
             kv_recv.at[half_at],
         )
@@ -288,7 +288,7 @@
         def _():
             kv_copy(0).start()
 
-        @pl.loop(1, rows_z)
+        @pl.loop(1, rows_h)
         def _(step):
             kv_copy(step).start()
 
@@ -302,7 +302,7 @@
         def _():
             kv_copy(0).wait_send()
 
-        @pl.loop(1, rows_z)
+        @pl.loop(1, rows_h)
         def _(step):
             kv_copy(step).wait_send()
 
@@ -350,17 +350,17 @@
         )
 
     def dkv_copy(which, at):
-        head = 2 * zl + (even if which == 0 else 1 - even)
+        head = 2 * row + (even if which == 0 else 1 - even)
         return remote(
             dkvown.at[which, :, lanes(at)],
             dkvfin.at[head],
             dkv_send.at[which, at],
             dkv_recv.at[head],
-            owner(core * part_size + at, x),
+            owner(core * part_size + at, line),
         )
 
     def dkv_start(which):
-        head = 2 * zl + (even if which == 0 else 1 - even)
+        head = 2 * row + (even if which == 0 else 1 - even)
 
         @pl.loop(0, part_size)
         def _(step):
@@ -413,9 +413,9 @@
         load.start()
 
     barrier = pltpu.get_barrier_semaphore()
-    peers = [owner(lax.rem(me + step, column), x) for step in range(1, column)]
-    peers += [owner(index, x + 1 - 2 * even) for index in range(column)]
-    peers += [across(offset) for offset in range(2, rows_x)]
+    peers = [owner(lax.rem(me + step, column), line) for step in range(1, column)]
+    peers += [owner(index, line + 1 - 2 * even) for index in range(column)]
+    peers += [across(offset) for offset in range(2, rows_k)]
     peers.append(partner)
     for peer in peers:
         pl.semaphore_signal(barrier, inc=1, device_id=peer, device_id_type=MESH)
@@ -509,16 +509,20 @@
     @pl.loop(0, part_size)
     def _(at):
         kv_arrived(at)
-        for offset in range(1, rows_x):
-            kvx_copy(offset, at).start()
         kvs_copy(0, at).start()
         kv_place(at).start()
 
-    @pl.loop(0, part_size)
-    def _(at):
-        for offset in range(1, rows_x):
-            kvx_copy(offset, at).wait_recv()
-            kvs_copy(offset, at).start()
+    for offset in range(1, rows_k):
+
+        @pl.loop(0, part_size)
+        def _(at):
+            kvx_copy(offset, at).start()
+
+    def take(block):
+        @pl.loop(0, part_size)
+        def _(at):
+            kvx_copy(block, at).wait_recv()
+            kvs_copy(block, at).start()
 
     def natural(block):
         lane = lax.broadcasted_iota(jnp.int32, (q_tile, padded), 1)
@@ -536,28 +540,26 @@
         qnat[rows, :] = qt[:, rows].astype(F32).T.astype(BF16)
         gnat[rows, :] = gt[:, rows].astype(F32).T
 
-    order = [0, 1, 3, 2]
-
-    def forward(block, is_first):
-        natural(block)
-
-        @pl.loop(0, span // q_tile)
-        def _(i):
-            rows = pl.ds(pl.multiple_of(i * q_tile, q_tile), q_tile)
-            scores = dot(qnat[rows, :], kv[block, :padded, :])
-            top = jnp.max(scores, -1, keepdims=True)
-            if not is_first:
-                before = tops[order[order.index(block) - 1], rows, :]
-                top = jnp.maximum(top, before)
-            tops[block, rows, :] = top
-            lifted = jnp.exp2((scores - top) * rate2).astype(BF16)
-            exps[block, rows, :] = lifted
-            term = dot(lifted, vnat[block])
-            if not is_first:
-                term += oacc[rows, :] * jnp.exp2((before - top) * rate2)
-            oacc[rows, :] = term
-
-    for n, block in enumerate(order):
+    order = [0, 1, 2, 3]
+    tiles = span // q_tile
+    middle_tile = (tiles - 1) // 2
+
+    def forward_rows(block, i):
+        rows = pl.ds(i * q_tile, q_tile)
+        scores = dot(qnat[rows, :], kv[block, :padded, :])
+        top = jnp.max(scores, -1, keepdims=True)
+        if block > 0:
+            before = tops[block - 1, rows, :]
+            top = jnp.maximum(top, before)
+        tops[block, rows, :] = top
+        lifted = jnp.exp2((scores - top) * rate2).astype(BF16)
+        exps[block, rows, :] = lifted
+        term = dot(lifted, vnat[block])
+        if block > 0:
+            term += oacc[rows, :] * jnp.exp2((before - top) * rate2)
+        oacc[rows, :] = term
+
+    for block in order:
 
         @pl.loop(0, part_size)
         def _(at):
@@ -565,7 +567,11 @@
             if block == 0:
                 kv_place(at).wait()
 
-        forward(block, n == 0)
+        natural(block)
+        for i in range(tiles):
+            forward_rows(block, i)
+            if i == middle_tile and block + 1 < rows_k:
+                take(block + 1)
 
     for at, size in spans(span, q_tile):
         rows = pl.ds(at, size)
@@ -575,7 +581,7 @@
         ot[:, rows] = mixed_values.T.astype(BF16)
         delta[rows, :] = jnp.sum(gnat[rows, :] * mixed_values, -1, keepdims=True)
         last = tops[order[-1], rows, :]
-        for block in range(rows_x):
+        for block in range(rows_k):
             lift = jnp.exp2((tops[block, rows, :] - last) * rate2)
             facs[block, rows, :] = lift * inverse
         qacc[rows, :] = jnp.zeros((size, padded), F32)
@@ -613,29 +619,26 @@
         dkvpart[block - 1] = total.astype(BF16)
         dkvx_copy(block).start()
 
-    turns = [2, 1, 3, 0]
+    turns = [2, 3, 1, 0]
     for n, block in enumerate(turns):
-        for i in range(span // q_tile):
+        for i in range(tiles):
             backward_rows(block, i)
-            if n > 0 and i == (span // q_tile - 1) // 2:
+            if n > 0 and i == middle_tile:
                 pass_on(turns[n - 1])
+            if block == 0:
+                rows = pl.ds(i * q_tile, q_tile)
+                dqt[:, rows] = (qacc[rows, :] * scale).T.astype(BF16)
+                for at in range(q_tile // CHUNK):
+                    back_one(DQ, i * (q_tile // CHUNK) + at, *dq_pair)
         dkvgive[block] = joined(1 - core).astype(BF16)
         dkvs_copy(block).start()
         keep[block] = joined(core)
 
-    for offset in (1, 3):
-        dkvx_copy(offset).wait_recv()
-    dkvown[1] = (dkvrecv[0].astype(F32) + dkvrecv[2].astype(F32)).astype(BF16)
-    dkv_start(1)
     dkvs_copy(0).wait_recv()
     dkvx_copy(2).wait_recv()
     total = keep[0] + dkvtake[0].astype(F32) + dkvrecv[1].astype(F32)
     dkvown[0] = total.astype(BF16)
     dkv_start(0)
-    for at, size in spans(span, q_tile):
-        rows = pl.ds(at, size)
-        dqt[:, rows] = (qacc[rows, :] * scale).T.astype(BF16)
-    back_start(DQ, *dq_pair)
 
     back_arrived(OUT, *o_pair)
     for head in range(column):
@@ -649,21 +652,34 @@
     out_store = pltpu.make_async_copy(outv, out_hbm, store_sem.at[0])
     out_store.start()
 
+    for offset in (1, 3):
+        dkvx_copy(offset).wait_recv()
+    dkvown[1] = (dkvrecv[0].astype(F32) + dkvrecv[2].astype(F32)).astype(BF16)
+    dkv_start(1)
+
+    def back_project(part):
+        rows = pl.ds(part * head_width, head_width)
+        gproj[part] = projt[rows, :].T.astype(BF16)
+
+    back_arrived(DQ, *dq_pair)
+    for head in range(column):
+        projt[pl.ds(head * depth, depth), :] = dqfin[head].astype(F32)[:depth]
+    back_project(0)
+    for at, size in spans(width, 512):
+        cols = pl.ds(at, size)
+        ginput[:, cols] = dot(gproj[0], win[pl.ds(0, head_width), cols])
     dkv_arrived()
     for head in range(column):
         both = dkvfin[head].astype(F32)
         projt[pl.ds(head_width + head * depth, depth), :] = both[:depth]
         projt[pl.ds(2 * head_width + head * depth, depth), :] = both[depth:]
-    back_arrived(DQ, *dq_pair)
-    for head in range(column):
-        projt[pl.ds(head * depth, depth), :] = dqfin[head].astype(F32)[:depth]
-    for part in range(3):
-        gproj[part] = projt[pl.ds(part * head_width, head_width), :].T.astype(BF16)
+    for part in (1, 2):
+        back_project(part)
     for at, size in spans(width, 512):
         cols = pl.ds(at, size)
-        ginput[:, cols] = sum(
+        ginput[:, cols] += sum(
             dot(gproj[part], win[pl.ds(part * head_width, head_width), cols])
-            for part in range(3)
+            for part in (1, 2)
         )
 
     def gm_copy(i):
@@ -723,12 +739,12 @@
     @pl.loop(0, part_size)
     def _(at):
         kvs_copy(0, at).wait_send()
-        for offset in range(1, rows_x):
+        for offset in range(1, rows_k):
             kvx_copy(offset, at).wait_send()
             kvs_copy(offset, at).wait_send()
 
     dkvs_copy(0).wait_send()
-    for offset in range(1, rows_x):
+    for offset in range(1, rows_k):
         dkvx_copy(offset).wait_send()
         dkvs_copy(offset).wait_send()
 
@@ -763,10 +779,10 @@
         copy.wait()
 
 
-def body(rows_z, rows_x, latents, skip_weight, project_in, project_out, upstream):
+def body(rows_h, rows_k, latents, skip_weight, project_in, project_out, upstream):
     tok, width = latents.shape[1:]
     head_width = project_out.shape[1]
-    column = rows_z * CORES
+    column = rows_h * CORES
     depth = head_width // column
     padded = depth + PAD
     span = column * tok
@@ -794,14 +810,14 @@
         vmem((column, padded, tok), BF16),
         vmem((padded, span), BF16),
         vmem((padded, span), BF16),
-        vmem((rows_x, 2 * depth, span), BF16),
-        vmem((rows_x, span, padded), BF16),
-        vmem((rows_x, span, padded), BF16),
+        vmem((rows_k, 2 * depth, span), BF16),
+        vmem((rows_k, span, padded), BF16),
+        vmem((rows_k, span, padded), BF16),
         vmem((span, padded), BF16),
         vmem((span, padded), F32),
-        vmem((rows_x, span, span), BF16),
-        vmem((rows_x, span, 1), F32),
-        vmem((rows_x, span, 1), F32),
+        vmem((rows_k, span, span), BF16),
+        vmem((rows_k, span, 1), F32),
+        vmem((rows_k, span, 1), F32),
         vmem((span, 1), F32),
         vmem((span, padded), F32),
         vmem((span, padded), F32),
@@ -809,11 +825,11 @@
         vmem((padded, span), BF16),
         vmem((padded, span), BF16),
         vmem((2, 2 * depth, part), BF16),
-        vmem((rows_x, 2 * depth, part), F32),
-        vmem((rows_x, 2 * depth, part), BF16),
-        vmem((rows_x, 2 * depth, part), BF16),
-        vmem((rows_x - 1, 2 * depth, part), BF16),
-        vmem((rows_x - 1, 2 * depth, part), BF16),
+        vmem((rows_k, 2 * depth, part), F32),
+        vmem((rows_k, 2 * depth, part), BF16),
+        vmem((rows_k, 2 * depth, part), BF16),
+        vmem((rows_k - 1, 2 * depth, part), BF16),
+        vmem((rows_k - 1, 2 * depth, part), BF16),
         vmem((2, 2 * depth, part), BF16),
         vmem((column, padded, tok), BF16),
         vmem((column, padded, tok), BF16),
@@ -828,26 +844,26 @@
         dma((2,)),
         dma((4, column)),
         dma((4, column)),
-        dma((rows_z,)),
+        dma((rows_h,)),
         dma((column // 2,)),
-        dma((rows_x - 1, column // 2)),
-        dma((rows_x - 1, column // 2)),
-        dma((rows_x, column // 2)),
-        dma((rows_x, column // 2)),
+        dma((rows_k - 1, column // 2)),
+        dma((rows_k - 1, column // 2)),
+        dma((rows_k, column // 2)),
+        dma((rows_k, column // 2)),
         dma((column // 2,)),
-        dma((rows_x,)),
-        dma((rows_x,)),
+        dma((rows_k,)),
+        dma((rows_k,)),
         dma((2, column // 2)),
         dma((column,)),
-        dma((rows_x - 1,)),
-        dma((rows_x - 1,)),
+        dma((rows_k - 1,)),
+        dma((rows_k - 1,)),
         dma((n_skip,)),
         dma((n_skip,)),
         dma((n_rows,)),
         dma((n_rows,)),
     ]
     out, glat = pl.pallas_call(
-        functools.partial(kernel, rows_z, rows_x),
+        functools.partial(kernel, rows_h, rows_k),
         out_shape=[jax.ShapeDtypeStruct(wide, BF16)] * 2,
         in_specs=[pl.BlockSpec(memory_space=pl.ANY)] * 5,
         out_specs=[pl.BlockSpec(memory_space=pl.ANY)] * 2,
@@ -868,10 +884,10 @@
 
 
 def solution(mesh):
-    rows_z = HEADS // CORES
-    rows_x = mesh.shape["seq"] // HEADS
+    rows_h = HEADS // 2
+    rows_k = mesh.shape["seq"] // HEADS
     return jax.shard_map(
-        functools.partial(body, rows_z, rows_x),
+        functools.partial(body, rows_h, rows_k),
         mesh=mesh,
         in_specs=(
             P("section", "seq", None),

time: 122 us -> 113 us (0.926)
  Pallas kernels: 121 us -> 112 us
    pallas_call x1, Pallas kernels: 119 us -> 110 us  [body(): pl.pallas_call(functools.partial(kernel, rows_h, rows_k), out_shape=[jax....]
where the time goes in v4:
time: 113 us
  Pallas kernels  112 us (99%)
    pallas_call x1, Pallas kernels, body(): pl.pallas_call(functools.partial(kernel, rows_h, rows_k), out_shape=[jax....  110 us

profile of v4, /device:TPU:33, one launch (start us, length us, event | category | flops | bytes accessed | tf_op | source)
XLA Modules:
  0.0 112.6 jit_solution(15492130757359906285)
XLA Ops:
  0.6 109.9 %shard_map.68 = (bf16[128,1408]{1,0:T(8,128)(2,1)}, bf16[128,1408]{1,0:T(8,128)(2,1)}) custom-call(bf16[128,1408]{1,0:T(8,128)(2,1)} %bitcast.12, bf16[1408,1408]{1,0:T(8,128)(2,1)} %bitcast.10, bf16[2112,1408]{1,0:T(8,128)(2,1)} %bitcast.9, bf16[704,1408]{1,0:T(8,128)(2,1)} %bitcast.11, bf16[128,1408]{1,0:T(8,128)(2,1)} %bitcast.13), custom_call_target="tpu_custom_call" | custom-call | tf_op jit(solution)/shard_map/pallas_call | solution.py:865
  110.6 1.9 %shard_map.69 = (bf16[128,1408]{1,0:T(8,128)(2,1)}, bf16[128,1408]{1,0:T(8,128)(2,1)}) custom-call(bf16[128,1408]{1,0:T(8,128)(2,1)} %get-tuple-element.6.out, bf16[128,1408]{1,0:T(8,128)(2,1)} %get-tuple-element.7.glat), custom_call_target="tpu_custom_call" | custom-call | tf_op jit(solution)/shard_map/pallas_call | solution.py:875

commit v5 on v4

--- a/solution.py
+++ b/solution.py
@@ -114,6 +114,7 @@
     dkv_recv,
     dkvx_send,
     dkvx_recv,
+    turn_sem,
     skip_ssem,
     skip_rsem,
     gm_ssem,
@@ -128,7 +129,6 @@
     is_upper = section >= sections // 2
     is_lower = jnp.logical_not(is_upper)
     column = rows_h * CORES
-    part_size = column // 2
     me = row * CORES + core
     even = lax.rem(line, 2)
     pair = line // 2
@@ -142,7 +142,8 @@
     span = column * CHUNK
     scale = 1.0 / math.sqrt(depth)
     rate2 = scale * math.log2(math.e)
-    q_tile = 256
+    q_tile = 512
+    half_span = span // 2
 
     def device(at_row, at_line, at_core):
         return {
@@ -258,35 +259,20 @@
             def _():
                 back_copy(kind, index, src, dst).wait_send()
 
-    half_core = me // part_size
-    half_at = lax.rem(me, part_size)
-    kv_mine = half_core == core
-
     def kv_copy(step):
-        at_row = lax.rem(row + step, rows_h)
+        there = lax.rem(row + step, rows_h)
         return remote(
-            kvsend.at[pl.ds(2 * at_row, 2)],
-            kvin.at[:, :, lanes(half_at)],
+            kvsend.at[pl.ds(2 * there, 2)],
+            kvin.at[:, :, lanes(row)],
             kv_send.at[step],
-            kv_recv.at[half_at],
-            device(at_row, line, half_core),
-        )
-
-    def kv_own():
-        return pltpu.make_async_copy(
-            kvsend.at[pl.ds(2 * row, 2)],
-            kvin.at[:, :, lanes(half_at)],
-            kv_recv.at[half_at],
+            kv_recv.at[row],
+            device(there, line, core),
         )
 
     def kv_start():
-        @pl.when(kv_mine)
-        def _():
-            kv_own().start()
-
-        @pl.when(jnp.logical_not(kv_mine))
-        def _():
-            kv_copy(0).start()
+        pltpu.make_async_copy(
+            kvsend.at[pl.ds(2 * row, 2)], kvin.at[:, :, lanes(row)], kv_recv.at[row]
+        ).start()
 
         @pl.loop(1, rows_h)
         def _(step):
@@ -298,16 +284,12 @@
         ).wait()
 
     def kv_sent():
-        @pl.when(jnp.logical_not(kv_mine))
-        def _():
-            kv_copy(0).wait_send()
-
         @pl.loop(1, rows_h)
         def _(step):
             kv_copy(step).wait_send()
 
     def half_lanes(at):
-        return lanes(core * part_size + at)
+        return lanes(core * rows_h + at)
 
     def kvx_copy(offset, at):
         head = even if offset == 2 else 1 - even
@@ -349,42 +331,31 @@
             across(offset),
         )
 
-    def dkv_copy(which, at):
+    def dkv_copy(which, step):
         head = 2 * row + (even if which == 0 else 1 - even)
+        there = lax.rem(row + step, rows_h)
         return remote(
-            dkvown.at[which, :, lanes(at)],
+            dkvown.at[which, :, lanes(there)],
             dkvfin.at[head],
-            dkv_send.at[which, at],
+            dkv_send.at[which, step],
             dkv_recv.at[head],
-            owner(core * part_size + at, line),
+            device(there, line, core),
         )
 
     def dkv_start(which):
         head = 2 * row + (even if which == 0 else 1 - even)
-
-        @pl.loop(0, part_size)
+        pltpu.make_async_copy(
+            dkvown.at[which, :, lanes(row)], dkvfin.at[head], dkv_recv.at[head]
+        ).start()
+
+        @pl.loop(1, rows_h)
         def _(step):
-            at = lax.rem(half_at + step, part_size)
-            mine = (step == 0) & kv_mine
-
-            @pl.when(mine)
-            def _():
-                pltpu.make_async_copy(
-                    dkvown.at[which, :, lanes(at)], dkvfin.at[head], dkv_recv.at[head]
-                ).start()
-
-            @pl.when(jnp.logical_not(mine))
-            def _():
-                dkv_copy(which, at).start()
+            dkv_copy(which, step).start()
 
     def dkv_sent(which):
-        @pl.loop(0, part_size)
+        @pl.loop(1, rows_h)
         def _(step):
-            at = lax.rem(half_at + step, part_size)
-
-            @pl.when((step > 0) | jnp.logical_not(kv_mine))
-            def _():
-                dkv_copy(which, at).wait_send()
+            dkv_copy(which, step).wait_send()
 
     def dkv_arrived():
         @pl.loop(0, column)
@@ -440,7 +411,7 @@
         if i == 0:
             pl.semaphore_wait(barrier, len(peers))
 
-        @pl.when(is_lower)
+        @pl.when(is_lower & (core == 0))
         def _():
             skip_copy(i).start()
 
@@ -462,6 +433,18 @@
         gsend[2 * i + 1] = jnp.concatenate([blank, two[depth:]], 0).astype(BF16)
 
     head_start(GRAD, *g_pair)
+
+    @pl.when(is_lower & (core == 0))
+    def _():
+        for i in range(len(skip_spans) - 1):
+            skip_copy(i).wait_send()
+        pl.semaphore_signal(turn_sem, inc=1, device_id=sibling, device_id_type=MESH)
+
+    @pl.when(is_lower & (core == 1))
+    def _():
+        pl.semaphore_wait(turn_sem, 1)
+        for i in range(len(skip_spans)):
+            skip_copy(i).start()
 
     row_spans = spans(tok, 32)
 
@@ -506,32 +489,27 @@
         qsend[head] = jnp.concatenate([queries, blank], 0).astype(BF16)
     head_start(QUERY, *q_pair)
 
-    @pl.loop(0, part_size)
+    @pl.loop(0, rows_h)
     def _(at):
         kv_arrived(at)
         kvs_copy(0, at).start()
         kv_place(at).start()
-
-    for offset in range(1, rows_k):
-
-        @pl.loop(0, part_size)
-        def _(at):
+        for offset in range(1, rows_k):
             kvx_copy(offset, at).start()
 
     def take(block):
-        @pl.loop(0, part_size)
+        @pl.loop(0, rows_h)
         def _(at):
             kvx_copy(block, at).wait_recv()
             kvs_copy(block, at).start()
 
-    def natural(block):
-        lane = lax.broadcasted_iota(jnp.int32, (q_tile, padded), 1)
-        for at, size in spans(span, q_tile):
-            cols = pl.ds(at, size)
-            keys = kv[block, :padded, cols].astype(F32).T
-            values = kv[block, depth - PAD :, cols].astype(F32).T
-            knat[block, cols, :] = keys.astype(BF16)
-            vnat[block, cols, :] = jnp.where(lane < PAD, 1.0, values).astype(BF16)
+    def natural(block, half):
+        lane = lax.broadcasted_iota(jnp.int32, (half_span, padded), 1)
+        cols = pl.ds(half * half_span, half_span)
+        keys = kv[block, :padded, cols].astype(F32).T
+        values = kv[block, depth - PAD :, cols].astype(F32).T
+        knat[block, cols, :] = keys.astype(BF16)
+        vnat[block, cols, :] = jnp.where(lane < PAD, 1.0, values).astype(BF16)
 
     head_arrived(GRAD, *g_pair)
     head_arrived(QUERY, *q_pair)
@@ -540,38 +518,59 @@
         qnat[rows, :] = qt[:, rows].astype(F32).T.astype(BF16)
         gnat[rows, :] = gt[:, rows].astype(F32).T
 
-    order = [0, 1, 2, 3]
     tiles = span // q_tile
     middle_tile = (tiles - 1) // 2
-
-    def forward_rows(block, i):
+    units = [(half, block) for half in range(2) for block in range(rows_k)]
+
+    def forward_rows(unit, i):
+        half, block = units[unit]
         rows = pl.ds(i * q_tile, q_tile)
-        scores = dot(qnat[rows, :], kv[block, :padded, :])
+        cols = pl.ds(half * half_span, half_span)
+        scores = dot(qnat[rows, :], kv[block, :padded, cols])
         top = jnp.max(scores, -1, keepdims=True)
-        if block > 0:
-            before = tops[block - 1, rows, :]
+        if unit > 0:
+            before = tops[unit - 1, rows, :]
             top = jnp.maximum(top, before)
-        tops[block, rows, :] = top
+        tops[unit, rows, :] = top
         lifted = jnp.exp2((scores - top) * rate2).astype(BF16)
-        exps[block, rows, :] = lifted
-        term = dot(lifted, vnat[block])
-        if block > 0:
+        exps[block, rows, cols] = lifted
+        term = dot(lifted, vnat[block, cols, :])
+        if unit > 0:
             term += oacc[rows, :] * jnp.exp2((before - top) * rate2)
         oacc[rows, :] = term
 
-    for block in order:
-
-        @pl.loop(0, part_size)
-        def _(at):
-            kvs_copy(block, at).wait_recv()
-            if block == 0:
-                kv_place(at).wait()
-
-        natural(block)
+    def await_half(half, block):
+        @pl.when(core != half)
+        def _():
+            @pl.loop(0, rows_h)
+            def _(at):
+                other = lanes((1 - core) * rows_h + at)
+                remote(
+                    kv.at[block, :, other],
+                    kv.at[block, :, other],
+                    kvs_send.at[block, at],
+                    kvs_recv.at[block, at],
+                    sibling,
+                ).wait_recv()
+
+        if block == 0:
+
+            @pl.when(core == half)
+            def _():
+                @pl.loop(0, rows_h)
+                def _(at):
+                    kv_place(at).wait()
+
+    for unit, (half, block) in enumerate(units):
+        await_half(half, block)
+        natural(block, half)
         for i in range(tiles):
-            forward_rows(block, i)
+            forward_rows(unit, i)
             if i == middle_tile and block + 1 < rows_k:
-                take(block + 1)
+
+                @pl.when(core == half)
+                def _():
+                    take(block + 1)
 
     for at, size in spans(span, q_tile):
         rows = pl.ds(at, size)
@@ -580,22 +579,23 @@
         mixed_values = (total * inverse).astype(BF16).astype(F32)
         ot[:, rows] = mixed_values.T.astype(BF16)
         delta[rows, :] = jnp.sum(gnat[rows, :] * mixed_values, -1, keepdims=True)
-        last = tops[order[-1], rows, :]
-        for block in range(rows_k):
-            lift = jnp.exp2((tops[block, rows, :] - last) * rate2)
-            facs[block, rows, :] = lift * inverse
+        last = tops[len(units) - 1, rows, :]
+        for unit in range(len(units)):
+            lift = jnp.exp2((tops[unit, rows, :] - last) * rate2)
+            facs[unit, rows, :] = lift * inverse
         qacc[rows, :] = jnp.zeros((size, padded), F32)
     back_start(OUT, *o_pair)
 
-    def backward_rows(block, i):
+    def backward_rows(half, block, i):
         rows = pl.ds(i * q_tile, q_tile)
-        factor = facs[block, rows, :]
+        cols = pl.ds(half * half_span, half_span)
+        factor = facs[units.index((half, block)), rows, :]
         grads = gnat[rows, :] * factor
         shift = delta[rows, :] * factor
-        lifted = exps[block, rows, :]
-        back = dot(grads.astype(BF16), kv[block, depth - PAD :, :]) - shift
+        lifted = exps[block, rows, cols]
+        back = dot(grads.astype(BF16), kv[block, depth - PAD :, cols]) - shift
         gscore = (lifted.astype(F32) * back).astype(BF16)
-        qacc[rows, :] += dot(gscore, knat[block])
+        qacc[rows, :] += dot(gscore, knat[block, cols, :])
         keys = dot(qt[:, rows], gscore)
         values = dot(grads.T.astype(BF16), lifted)
         if i > 0:
@@ -604,12 +604,9 @@
         kvacc[:padded, :] = keys
         kvacc[padded:, :] = values
 
-    half_span = span // 2
-
-    def joined(which):
-        cols = pl.ds(pl.multiple_of(which * half_span, CHUNK), half_span)
-        keys = kvacc[:padded, cols] * scale
-        values = kvacc[padded:, cols]
+    def joined():
+        keys = kvacc[:padded, :] * scale
+        values = kvacc[padded:, :]
         middle = keys[depth - PAD :] + values[: 2 * PAD]
         return jnp.concatenate([keys[: depth - PAD], middle, values[2 * PAD :]], 0)
 
@@ -619,20 +616,31 @@
         dkvpart[block - 1] = total.astype(BF16)
         dkvx_copy(block).start()
 
-    turns = [2, 3, 1, 0]
-    for n, block in enumerate(turns):
+    turns = [(half, block) for half in range(2) for block in (2, 3, 1, 0)]
+    for n, (half, block) in enumerate(turns):
         for i in range(tiles):
-            backward_rows(block, i)
-            if n > 0 and i == middle_tile:
-                pass_on(turns[n - 1])
-            if block == 0:
+            backward_rows(half, block, i)
+            if n > 0 and i == middle_tile and turns[n - 1][1] > 0:
+                half_before, block_before = turns[n - 1]
+
+                @pl.when(core == half_before)
+                def _():
+                    pass_on(block_before)
+
+            if n == len(turns) - 1:
                 rows = pl.ds(i * q_tile, q_tile)
                 dqt[:, rows] = (qacc[rows, :] * scale).T.astype(BF16)
                 for at in range(q_tile // CHUNK):
                     back_one(DQ, i * (q_tile // CHUNK) + at, *dq_pair)
-        dkvgive[block] = joined(1 - core).astype(BF16)
-        dkvs_copy(block).start()
-        keep[block] = joined(core)
+
+        @pl.when(core != half)
+        def _():
+            dkvgive[block] = joined().astype(BF16)
+            dkvs_copy(block).start()
+
+        @pl.when(core == half)
+        def _():
+            keep[block] = joined()
 
     dkvs_copy(0).wait_recv()
     dkvx_copy(2).wait_recv()
@@ -736,7 +744,7 @@
     dkv_sent(0)
     dkv_sent(1)
 
-    @pl.loop(0, part_size)
+    @pl.loop(0, rows_h)
     def _(at):
         kvs_copy(0, at).wait_send()
         for offset in range(1, rows_k):
@@ -748,7 +756,11 @@
         dkvx_copy(offset).wait_send()
         dkvs_copy(offset).wait_send()
 
-    @pl.when(is_lower)
+    @pl.when(is_lower & (core == 0))
+    def _():
+        skip_copy(len(skip_spans) - 1).wait_send()
+
+    @pl.when(is_lower & (core == 1))
     def _():
         for i in range(len(skip_spans)):
             skip_copy(i).wait_send()
@@ -816,12 +828,12 @@
         vmem((span, padded), BF16),
         vmem((span, padded), F32),
         vmem((rows_k, span, span), BF16),
-        vmem((rows_k, span, 1), F32),
-        vmem((rows_k, span, 1), F32),
+        vmem((2 * rows_k, span, 1), F32),
+        vmem((2 * rows_k, span, 1), F32),
         vmem((span, 1), F32),
         vmem((span, padded), F32),
         vmem((span, padded), F32),
-        vmem((2 * padded, span), F32),
+        vmem((2 * padded, part), F32),
         vmem((padded, span), BF16),
         vmem((padded, span), BF16),
         vmem((2, 2 * depth, part), BF16),
@@ -857,6 +869,7 @@
         dma((column,)),
         dma((rows_k - 1,)),
         dma((rows_k - 1,)),
+        pltpu.SemaphoreType.REGULAR,
         dma((n_skip,)),
         dma((n_skip,)),
         dma((n_rows,)),

time: 113 us -> 118 us (1.044)
  Pallas kernels: 112 us -> 117 us
    pallas_call x1, Pallas kernels: 110 us -> 115 us  [body(): pl.pallas_call(functools.partial(kernel, rows_h, rows_k), out_shape=[jax....]
where the time goes in v5:
time: 118 us
  Pallas kernels  117 us (99%)
    pallas_call x1, Pallas kernels, body(): pl.pallas_call(functools.partial(kernel, rows_h, rows_k), out_shape=[jax....  115 us

profile of v5, /device:TPU:33, one launch (start us, length us, event | category | flops | bytes accessed | tf_op | source)
XLA Modules:
  0.0 118.0 jit_solution(2398507342644326106)
XLA Ops:
  0.6 115.3 %shard_map.68 = (bf16[128,1408]{1,0:T(8,128)(2,1)}, bf16[128,1408]{1,0:T(8,128)(2,1)}) custom-call(bf16[128,1408]{1,0:T(8,128)(2,1)} %bitcast.12, bf16[1408,1408]{1,0:T(8,128)(2,1)} %bitcast.10, bf16[2112,1408]{1,0:T(8,128)(2,1)} %bitcast.9, bf16[704,1408]{1,0:T(8,128)(2,1)} %bitcast.11, bf16[128,1408]{1,0:T(8,128)(2,1)} %bitcast.13), custom_call_target="tpu_custom_call" | custom-call | tf_op jit(solution)/shard_map/pallas_call | solution.py:878
  116.0 1.9 %shard_map.69 = (bf16[128,1408]{1,0:T(8,128)(2,1)}, bf16[128,1408]{1,0:T(8,128)(2,1)}) custom-call(bf16[128,1408]{1,0:T(8,128)(2,1)} %get-tuple-element.6.out, bf16[128,1408]{1,0:T(8,128)(2,1)} %get-tuple-element.7.glat), custom_call_target="tpu_custom_call" | custom-call | tf_op jit(solution)/shard_map/pallas_call | solution.py:888

commit v6 on v4

--- a/solution.py
+++ b/solution.py
@@ -122,8 +122,8 @@
     sections = lax.axis_size("section")
     section = lax.axis_index("section")
     place = lax.axis_index("seq")
-    line = place // (rows_h * CORES)
-    row = lax.rem(place // CORES, rows_h)
+    row = place // (rows_k * CORES)
+    line = lax.rem(place // CORES, rows_k)
     core = lax.rem(place, CORES)
     is_upper = section >= sections // 2
     is_lower = jnp.logical_not(is_upper)
@@ -147,7 +147,7 @@
     def device(at_row, at_line, at_core):
         return {
             "section": section,
-            "seq": (at_line * rows_h + at_row) * CORES + at_core,
+            "seq": (at_row * rows_k + at_line) * CORES + at_core,
         }
 
     def owner(index, at_line):
@@ -461,7 +461,10 @@
         gsend[2 * i] = jnp.concatenate([blank, two[:depth]], 0).astype(BF16)
         gsend[2 * i + 1] = jnp.concatenate([blank, two[depth:]], 0).astype(BF16)
 
-    head_start(GRAD, *g_pair)
+    @pl.when(is_lower)
+    def _():
+        for i in range(len(skip_spans)):
+            skip_copy(i).wait_send()
 
     row_spans = spans(tok, 32)
 
@@ -505,6 +508,7 @@
         queries = projt[pl.ds(head * depth, depth), :]
         qsend[head] = jnp.concatenate([queries, blank], 0).astype(BF16)
     head_start(QUERY, *q_pair)
+    head_start(GRAD, *g_pair)
 
     @pl.loop(0, part_size)
     def _(at):
@@ -533,12 +537,10 @@
             knat[block, cols, :] = keys.astype(BF16)
             vnat[block, cols, :] = jnp.where(lane < PAD, 1.0, values).astype(BF16)
 
-    head_arrived(GRAD, *g_pair)
     head_arrived(QUERY, *q_pair)
     for at, size in spans(span, q_tile):
         rows = pl.ds(at, size)
         qnat[rows, :] = qt[:, rows].astype(F32).T.astype(BF16)
-        gnat[rows, :] = gt[:, rows].astype(F32).T
 
     order = [0, 1, 2, 3]
     tiles = span // q_tile
@@ -573,8 +575,10 @@
             if i == middle_tile and block + 1 < rows_k:
                 take(block + 1)
 
+    head_arrived(GRAD, *g_pair)
     for at, size in spans(span, q_tile):
         rows = pl.ds(at, size)
+        gnat[rows, :] = gt[:, rows].astype(F32).T
         total = oacc[rows, :]
         inverse = 1.0 / total[:, :1]
         mixed_values = (total * inverse).astype(BF16).astype(F32)
@@ -747,11 +751,6 @@
     for offset in range(1, rows_k):
         dkvx_copy(offset).wait_send()
         dkvs_copy(offset).wait_send()
-
-    @pl.when(is_lower)
-    def _():
-        for i in range(len(skip_spans)):
-            skip_copy(i).wait_send()
 
     @pl.when(is_upper)
     def _():

time: 113 us -> 109 us (0.965)
  Pallas kernels: 112 us -> 108 us
    pallas_call x1, Pallas kernels: 110 us -> 106 us  [body(): pl.pallas_call(functools.partial(kernel, rows_h, rows_k), out_shape=[jax....]
where the time goes in v6:
time: 109 us
  Pallas kernels  108 us (99%)
    pallas_call x1, Pallas kernels, body(): pl.pallas_call(functools.partial(kernel, rows_h, rows_k), out_shape=[jax....  106 us

profile of v6, /device:TPU:33, one launch (start us, length us, event | category | flops | bytes accessed | tf_op | source)
XLA Modules:
  0.0 108.9 jit_solution(3110855450797071125)
XLA Ops:
  0.6 106.2 %shard_map.68 = (bf16[128,1408]{1,0:T(8,128)(2,1)}, bf16[128,1408]{1,0:T(8,128)(2,1)}) custom-call(bf16[128,1408]{1,0:T(8,128)(2,1)} %bitcast.12, bf16[1408,1408]{1,0:T(8,128)(2,1)} %bitcast.10, bf16[2112,1408]{1,0:T(8,128)(2,1)} %bitcast.9, bf16[704,1408]{1,0:T(8,128)(2,1)} %bitcast.11, bf16[128,1408]{1,0:T(8,128)(2,1)} %bitcast.13), custom_call_target="tpu_custom_call" | custom-call | tf_op jit(solution)/shard_map/pallas_call | solution.py:864
  106.9 1.9 %shard_map.69 = (bf16[128,1408]{1,0:T(8,128)(2,1)}, bf16[128,1408]{1,0:T(8,128)(2,1)}) custom-call(bf16[128,1408]{1,0:T(8,128)(2,1)} %get-tuple-element.6.out, bf16[128,1408]{1,0:T(8,128)(2,1)} %get-tuple-element.7.glat), custom_call_target="tpu_custom_call" | custom-call | tf_op jit(solution)/shard_map/pallas_call | solution.py:874

commit v7 on v6

--- a/solution.py
+++ b/solution.py
@@ -542,7 +542,7 @@
         rows = pl.ds(at, size)
         qnat[rows, :] = qt[:, rows].astype(F32).T.astype(BF16)
 
-    order = [0, 1, 2, 3]
+    order = [0, 1, 3, 2]
     tiles = span // q_tile
     middle_tile = (tiles - 1) // 2
 
@@ -551,7 +551,7 @@
         scores = dot(qnat[rows, :], kv[block, :padded, :])
         top = jnp.max(scores, -1, keepdims=True)
         if block > 0:
-            before = tops[block - 1, rows, :]
+            before = tops[order[order.index(block) - 1], rows, :]
             top = jnp.maximum(top, before)
         tops[block, rows, :] = top
         lifted = jnp.exp2((scores - top) * rate2).astype(BF16)
@@ -572,8 +572,8 @@
         natural(block)
         for i in range(tiles):
             forward_rows(block, i)
-            if i == middle_tile and block + 1 < rows_k:
-                take(block + 1)
+            if i == middle_tile and block != order[-1]:
+                take(order[order.index(block) + 1])
 
     head_arrived(GRAD, *g_pair)
     for at, size in spans(span, q_tile):

time: 109 us -> 107 us (0.982)
  Pallas kernels: 108 us -> 106 us
    pallas_call x1, Pallas kernels: 106 us -> 104 us  [body(): pl.pallas_call(functools.partial(kernel, rows_h, rows_k), out_shape=[jax....]
where the time goes in v7:
time: 107 us
  Pallas kernels  106 us (99%)
    pallas_call x1, Pallas kernels, body(): pl.pallas_call(functools.partial(kernel, rows_h, rows_k), out_shape=[jax....  104 us

profile of v7, /device:TPU:33, one launch (start us, length us, event | category | flops | bytes accessed | tf_op | source)
XLA Modules:
  0.0 106.7 jit_solution(8409540231012931342)
XLA Ops:
  0.6 104.0 %shard_map.68 = (bf16[128,1408]{1,0:T(8,128)(2,1)}, bf16[128,1408]{1,0:T(8,128)(2,1)}) custom-call(bf16[128,1408]{1,0:T(8,128)(2,1)} %bitcast.12, bf16[1408,1408]{1,0:T(8,128)(2,1)} %bitcast.10, bf16[2112,1408]{1,0:T(8,128)(2,1)} %bitcast.9, bf16[704,1408]{1,0:T(8,128)(2,1)} %bitcast.11, bf16[128,1408]{1,0:T(8,128)(2,1)} %bitcast.13), custom_call_target="tpu_custom_call" | custom-call | tf_op jit(solution)/shard_map/pallas_call | solution.py:864
  104.6 1.9 %shard_map.69 = (bf16[128,1408]{1,0:T(8,128)(2,1)}, bf16[128,1408]{1,0:T(8,128)(2,1)}) custom-call(bf16[128,1408]{1,0:T(8,128)(2,1)} %get-tuple-element.6.out, bf16[128,1408]{1,0:T(8,128)(2,1)} %get-tuple-element.7.glat), custom_call_target="tpu_custom_call" | custom-call | tf_op jit(solution)/shard_map/pallas_call | solution.py:874

commit v8 on v7

--- a/solution.py
+++ b/solution.py
@@ -544,7 +544,7 @@
 
     order = [0, 1, 3, 2]
     tiles = span // q_tile
-    middle_tile = (tiles - 1) // 2
+    middle_tile = tiles // 2
 
     def forward_rows(block, i):
         rows = pl.ds(i * q_tile, q_tile)

time: 107 us -> 108 us (level)
  no operation moved by 1% of the time
where the time goes in v8:
time: 108 us
  Pallas kernels  107 us (99%)
    pallas_call x1, Pallas kernels, body(): pl.pallas_call(functools.partial(kernel, rows_h, rows_k), out_shape=[jax....  105 us

profile of v8, /device:TPU:33, one launch (start us, length us, event | category | flops | bytes accessed | tf_op | source)
XLA Modules:
  0.0 107.6 jit_solution(14713112489654439384)
XLA Ops:
  0.6 104.9 %shard_map.68 = (bf16[128,1408]{1,0:T(8,128)(2,1)}, bf16[128,1408]{1,0:T(8,128)(2,1)}) custom-call(bf16[128,1408]{1,0:T(8,128)(2,1)} %bitcast.12, bf16[1408,1408]{1,0:T(8,128)(2,1)} %bitcast.10, bf16[2112,1408]{1,0:T(8,128)(2,1)} %bitcast.9, bf16[704,1408]{1,0:T(8,128)(2,1)} %bitcast.11, bf16[128,1408]{1,0:T(8,128)(2,1)} %bitcast.13), custom_call_target="tpu_custom_call" | custom-call | tf_op jit(solution)/shard_map/pallas_call | solution.py:864
  105.5 1.9 %shard_map.69 = (bf16[128,1408]{1,0:T(8,128)(2,1)}, bf16[128,1408]{1,0:T(8,128)(2,1)}) custom-call(bf16[128,1408]{1,0:T(8,128)(2,1)} %get-tuple-element.6.out, bf16[128,1408]{1,0:T(8,128)(2,1)} %get-tuple-element.7.glat), custom_call_target="tpu_custom_call" | custom-call | tf_op jit(solution)/shard_map/pallas_call | solution.py:874
